TPU v7x, 128 devices: a whole 4x4x4 slice. The times are simulated.
128 devices in a mesh: seq: 16 (over y, x_hi, core), head: 4 (over z), dp: 2 (over x_lo).
Axes of the slice: x: 4 (x_hi: 2, x_lo: 2; x = x_hi * 2 + x_lo), y: 4, z: 4, core: 2. Of those that a mesh axis runs over, the one named last changes fastest.
Arguments:
- inputs_x: bfloat16 [2, 16384, 8192], P('dp', 'seq', 'head'), may hold values from -6 to 6
- inputs_bc: bfloat16 [2, 16384, 256], P('dp', 'seq'), may hold values from -9 to 9
- dt_raw: float32 [2, 16384, 128], P('dp', 'seq', 'head'), may hold values from -14 to 0
- grad_out: bfloat16 [2, 16384, 8192], P('dp', 'seq', 'head'), may hold values from -12 to 12
- a_log: float32 [128], P('head'), may hold values from 0 to 0.7
- dt_bias: float32 [128], P('head'), may hold values from -0.3 to 0.3
- skip: float32 [128], P('head'), may hold values from 0.5 to 1.5
Outputs:
- grad_x: bfloat16 [2, 16384, 8192], P('dp', 'seq', 'head')
- grad_bc: float32 [2, 16384, 256], P('dp', 'seq')
- grad_dt: float32 [2, 16384, 128], P('dp', 'seq', 'head')
- grad_heads: float32 [3, 128], P(None, 'head')
All inputs are finite; a program needn't handle non-finite values.
Results may differ from a plain program's by a relative error of at most 0.0014.
Values sent between devices are 32-bit elements; how exact they have to be, the bound alone decides.
A program may use at most 192 MiB of HBM per device.

v0:
```python
import math

import jax
import jax.numpy as jnp
from jax import lax
from jax.sharding import PartitionSpec as P

GROUP = 256


HIGH = lax.Precision.HIGHEST


def carried_in(array, axis, combine, identity, reverse):
    count, place = (lax.axis_size(axis), lax.axis_index(axis))
    everything = jax.tree.map(lambda part: lax.all_gather(part, axis), array)
    start = jax.tree.map(
        lambda part, zero: jnp.broadcast_to(jnp.asarray(zero, part.dtype), part.shape),
        array,
        identity,
    )

    def hop(k, before):
        at = count - 1 - k if reverse else k
        reached = at > place if reverse else at < place
        new = combine(before, jax.tree.map(lambda part: part[at], everything))
        return jax.tree.map(lambda a, b: jnp.where(reached, a, b), new, before)

    return lax.fori_loop(0, count, hop, start)


def link(earlier, later):
    return (earlier[0] + later[0], jnp.exp(later[0])[:, None, None] * earlier[1] + later[1])


def block_grads(x_half, y_half, b_half, c_half, xf, yf, bmat, cmat, dtv, cum, hin, gout):
    size = cum.shape[0]
    lower = (jnp.arange(size)[:, None] >= jnp.arange(size)[None, :])[:, :, None]
    gap = cum[:, None, :] - cum[None, :, :]
    decay = jnp.where(lower, jnp.exp(jnp.where(lower, gap, 0.0)), 0.0)
    xs = xf * dtv[:, :, None]
    scores = jnp.dot(c_half, b_half.T, preferred_element_type=jnp.float32)
    paired = jnp.einsum("ihp,jhp->ijh", y_half, x_half, preferred_element_type=jnp.float32) * (
        dtv[None, :, :] * decay
    )
    weight = scores[:, :, None] * decay
    wend = jnp.exp(cum[-1][None, :] - cum)
    spread = jnp.einsum("hpn,jn->jhp", gout, bmat, precision=HIGH)
    dxs = jnp.einsum("ijh,ihp->jhp", weight, yf, precision=HIGH) + wend[:, :, None] * spread
    summed = jnp.sum(paired, axis=2)
    grad_b = jnp.dot(summed.T, cmat, precision=HIGH) + jnp.einsum(
        "jhp,hpn->jn", xs * wend[:, :, None], gout, precision=HIGH
    )
    lifted = yf * jnp.exp(cum)[:, :, None]
    grad_c = jnp.dot(summed, bmat, precision=HIGH) + jnp.einsum(
        "ihp,hpn->in", lifted, hin, precision=HIGH
    )
    inner = scores[:, :, None] * paired
    edge = wend * jnp.sum(xs * spread, axis=2)
    carried = jnp.einsum("in,hpn->ihp", cmat, hin, precision=HIGH)
    dcum = (
        jnp.sum(inner, axis=1) - jnp.sum(inner, axis=0) + jnp.sum(lifted * carried, axis=2) - edge
    )
    closing = jnp.exp(cum[-1]) * jnp.sum(gout * hin, axis=(1, 2)) + jnp.sum(edge, axis=0)
    dcum = dcum.at[size - 1].add(closing)
    dlog = jnp.flip(jnp.cumsum(jnp.flip(dcum, 0), axis=0), 0)
    return (dxs, grad_b, grad_c, dlog, lifted)


def shards(inputs_x, inputs_bc, dt_raw, grad_out, a_log, dt_bias, skip):
    length = inputs_x.shape[1]
    heads = a_log.shape[0]
    width = inputs_x.shape[2]
    headdim = width // heads
    state = inputs_bc.shape[2] // 2
    blocks = length // GROUP
    rate = -jnp.exp(a_log)
    shifted = dt_raw[0] + dt_bias[None, :]
    step_dt = jax.nn.softplus(shifted)
    cumul = jnp.cumsum((step_dt * rate[None, :]).reshape(blocks, GROUP, heads), axis=1)
    x_blocks = inputs_x[0].reshape(blocks, GROUP, heads, headdim)
    y_blocks = grad_out[0].reshape(blocks, GROUP, heads, headdim)
    b_half = inputs_bc[0, :, :state].reshape(blocks, GROUP, state)
    c_half = inputs_bc[0, :, state:].reshape(blocks, GROUP, state)
    b_blocks = b_half.astype(jnp.float32)
    c_blocks = c_half.astype(jnp.float32)
    dt_blocks = step_dt.reshape(blocks, GROUP, heads)

    def local_terms(operands):
        x_blk, y_blk, b_blk, c_blk, dt_blk, cum_blk = operands
        xs = x_blk.astype(jnp.float32) * dt_blk[:, :, None]
        wend = jnp.exp(cum_blk[-1][None, :] - cum_blk)
        ends = jnp.einsum("qhp,qn->hpn", xs * wend[:, :, None], b_blk, precision=HIGH)
        lifted = y_blk.astype(jnp.float32) * jnp.exp(cum_blk)[:, :, None]
        starts = jnp.einsum("qhp,qn->hpn", lifted, c_blk, precision=HIGH)
        return (ends, starts)

    ends, starts = lax.map(local_terms, (x_blocks, y_blocks, b_blocks, c_blocks, dt_blocks, cumul))
    lasts = cumul[:, -1, :]
    dev_state = jnp.zeros((heads, headdim, state), jnp.float32)
    dev_grad = jnp.zeros((heads, headdim, state), jnp.float32)
    for index in range(blocks):
        dev_state = jnp.exp(lasts[index])[:, None, None] * dev_state + ends[index]
    for index in reversed(range(blocks)):
        dev_grad = jnp.exp(lasts[index])[:, None, None] * dev_grad + starts[index]
    dev_log = jnp.sum(lasts, axis=0)
    neutral = (jnp.zeros_like(dev_log), jnp.zeros_like(dev_state))
    incoming = carried_in((dev_log, dev_state), "seq", link, neutral, False)[1]
    outgoing = carried_in((dev_log, dev_grad), "seq", link, neutral, True)[1]
    entering = []
    current = incoming
    for index in range(blocks):
        entering.append(current)
        current = jnp.exp(lasts[index])[:, None, None] * current + ends[index]
    leaving = [current] * blocks
    current = outgoing
    for index in reversed(range(blocks)):
        leaving[index] = current
        current = jnp.exp(lasts[index])[:, None, None] * current + starts[index]

    def full_terms(operands):
        x_blk, y_blk, bh_blk, ch_blk, b_blk, c_blk, dt_blk, cum_blk, hin, gout = operands
        xf = x_blk.astype(jnp.float32)
        yf = y_blk.astype(jnp.float32)
        dxs, grad_b, grad_c, dlog, lifted = block_grads(
            x_blk, y_blk, bh_blk, ch_blk, xf, yf, b_blk, c_blk, dt_blk, cum_blk, hin, gout
        )
        grad_x = dxs * dt_blk[:, :, None] + skip[None, :, None] * yf
        grad_step = jnp.sum(dxs * xf, axis=2) + dlog * rate[None, :]
        return (grad_x.reshape(GROUP, width).astype(jnp.bfloat16), grad_b, grad_c, grad_step, dlog)

    grad_x, part_b, part_c, grad_step, dlog = lax.map(
        full_terms,
        (
            x_blocks,
            y_blocks,
            b_half,
            c_half,
            b_blocks,
            c_blocks,
            dt_blocks,
            cumul,
            jnp.stack(entering),
            jnp.stack(leaving),
        ),
    )
    total_b, total_c = lax.psum(
        (part_b.reshape(length, state), part_c.reshape(length, state)), "head"
    )
    grad_bc = jnp.concatenate([total_b, total_c], axis=1)[None]
    grad_dt = grad_step.reshape(length, heads) * jax.nn.sigmoid(shifted)
    dlog = dlog.reshape(length, heads)
    d_alog = jnp.sum(dlog * step_dt, axis=0) * rate
    d_bias = jnp.sum(grad_dt, axis=0)
    d_skip = jnp.sum(
        jnp.einsum(
            "tc,tc->c", grad_out[0], inputs_x[0], preferred_element_type=jnp.float32
        ).reshape(heads, headdim),
        axis=1,
    )
    sequences = inputs_x.shape[0] * lax.axis_size("dp")
    scale = 1.0 / math.sqrt(sequences * length * lax.axis_size("seq"))
    grad_heads = lax.psum(jnp.stack([d_alog, d_bias, d_skip]), ("seq", "dp")) * scale
    return (grad_x.reshape(1, length, width), grad_bc, grad_dt[None], grad_heads)


def solution(mesh):
    placed = (
        P("dp", "seq", "head"),
        P("dp", "seq", None),
        P("dp", "seq", "head"),
        P("dp", "seq", "head"),
        P("head"),
        P("head"),
        P("head"),
    )
    return jax.shard_map(
        shards,
        mesh=mesh,
        in_specs=placed,
        out_specs=(
            P("dp", "seq", "head"),
            P("dp", "seq", None),
            P("dp", "seq", "head"),
            P(None, "head"),
        ),
        check_vma=False,
    )
```

profile of v0, /device:TPU:0, one launch (start us, length us, event | category | flops | bytes accessed | tf_op | source)
XLA Modules:
  0.0 619.4 jit_solution(8284108192951843389)
XLA Ops:
  17.4 12.9 %reshape.327 = bf16[4,256,32,64]{3,2,1,0:T(8,128)(2,1)} reshape(bf16[1,1024,2048]{2,1,0:T(8,128)(2,1)} %param.17) | data formatting | bytes 8388608 | tf_op jit(solution)/shard_map/reshape;squeeze | solution.py:81
  30.3 10.4 %copy.152 = bf16[4,256,32,64]{1,3,2,0:T(8,128)(2,1)} copy(bf16[4,256,32,64]{3,2,1,0:T(8,128)(2,1)} %reshape.327) | data formatting | bytes 8388608 | tf_op jit(solution)/shard_map/while | solution.py:98
  40.6 12.9 %reshape.326 = bf16[4,256,32,64]{3,2,1,0:T(8,128)(2,1)} reshape(bf16[1,1024,2048]{2,1,0:T(8,128)(2,1)} %param.20) | data formatting | bytes 8388608 | tf_op jit(solution)/shard_map/reshape;squeeze | solution.py:82
  53.5 10.3 %copy.157 = bf16[4,256,32,64]{1,3,2,0:T(8,128)(2,1)} copy(bf16[4,256,32,64]{3,2,1,0:T(8,128)(2,1)} %reshape.326) | data formatting | bytes 8388608 | tf_op jit(solution)/shard_map/while | solution.py:132
  63.8 36.4 %while.67 = (s32[]{:T(128)}, f32[4,32,64,128]{3,2,1,0:T(8,128)}, f32[4,32,64,128]{3,2,1,0:T(8,128)}, bf16[4,256,32,64]{1,3,2,0:T(8,128)(2,1)}, f32[4,256,32]{1,2...) while((s32[]{:T(128)}, f32[4,32,64,128]{3,2,1,0:T(8,128)}, ...), condition=%wide.region_4.5_spmd.clone, body=%wide.region_3.4_spmd.sunk.clone | while | flops 1613242368 | bytes 4722169 | solution.py:98
  100.3 5.3 slice_add_fusion.1
  108.2 38.7 %all-reduce = f32[512]{0:T(512)S(1)} all-reduce(f32[512]{0:T(512)S(1)} %dynamic-update-slice.6), channel_id=2, replica_groups=mesh['seq'=16,'head'=4,'dp'=2] {'seq'}, use_global_device_ids=true, to_apply=%add | all-reduce | flops 512 | bytes 4096
  147.0 5.2 fusion.115
  152.4 65.3 %all-gather.6.cloned.1.call-done = f32[16,32,64,128]{3,2,1,0:T(8,128)} async-done(((f32[1,32,64,128]{3,2,1,0:T(8,128)}), f32[16,32,64,128]{3,2,1,0:T(8,128)}) %all-gather.6.cloned.1.call-update) | async-done | bytes 16777232 | tf_op jit(solution)/shard_map/all_gather | solution.py:16
  217.7 24.3 %while.70 = (s32[]{:T(128)}, f32[32,64,128]{2,1,0:T(8,128)S(1)}, s32[]{:T(128)}, f32[16,32]{1,0:T(8,128)S(1)}, f32[16,32,64,128]{3,2,1,0:T(8,128)}) while((s32[]{:T(128)}, f32[32,64,128]{2,1,0:T(8,128)S(1)}, s32[]{:T(128)}, f32[16,32]{1,0:T(8,128)S(1)}, f32[16,32,64,128]{3,2,1,0:T(8,128)}) %tuple.175), condition=%wide.region_6.7_spmd.clone.clone, body=%wide.region_5.6_spmd.clone.sunk.clone | while | flops 1048580 | bytes 3146201 | solution.py:29
  242.1 85.0 %all-gather.4.cloned.1.call-done = f32[16,32,64,128]{3,2,1,0:T(8,128)} async-done(((f32[1,32,64,128]{3,2,1,0:T(8,128)}), f32[16,32,64,128]{3,2,1,0:T(8,128)}) %all-gather.4.cloned.1.call-update) | async-done | bytes 16777232 | tf_op jit(solution)/shard_map/all_gather | solution.py:16
  327.1 24.2 %while.69 = (s32[]{:T(128)}, f32[32,64,128]{2,1,0:T(8,128)S(1)}, s32[]{:T(128)}, f32[16,32]{1,0:T(8,128)S(1)}, f32[16,32,64,128]{3,2,1,0:T(8,128)}) while((s32[]{:T(128)}, f32[32,64,128]{2,1,0:T(8,128)S(1)}, s32[]{:T(128)}, f32[16,32]{1,0:T(8,128)S(1)}, f32[16,32,64,128]{3,2,1,0:T(8,128)}) %tuple.193), condition=%wide.region_8.9_spmd.clone.clone, body=%wide.region_7.8_spmd.clone.sunk.clone | while | flops 1048584 | bytes 3146247 | solution.py:29
  359.7 181.0 %while.68 = (s32[]{:T(128)}, bf16[4,256,2048]{2,1,0:T(8,128)(2,1)}, f32[4,256,128]{2,1,0:T(8,128)}, f32[4,256,128]{2,1,0:T(8,128)}, f32[4,256,32]{1,0,2:T(4,128)...) while((s32[]{:T(128)}, bf16[4,256,2048]{2,1,0:T(8,128)(2,1)}, ...), condition=%wide.region_20.21_spmd.clone, body=%wide.region_9.0_spmd.sunk.clone | while | flops 5358837760 | bytes 30554368 | solution.py:132
  364.9 8.8 %fusion.218 = (f32[256,32]{0,1:T(8,128)S(1)}, f32[256,32]{0,1:T(8,128)S(1)}, bf16[256,32,64]{0,2,1:T(8,128)(2,1)S(1)}) fusion(f32[256,32,64]{0,2,1:T(8,128)S(1)} %fusion.215, f32[256,32]{0,1:T(8,128)S(1)} %dynamic-slice_bitcast_fusion.7, bf16[4,256,32,64]{1,3,2,0:T(8,128)(2,1)} %get-tuple-element.1292, s32[]{:T(128)} %get-tuple-element.1260, ...), kind=kOutput, calls=%fused_computation.56.clone.1.clone | convolution fusion | flops 1625800704 | bytes 6817280 | tf_op jit(solution)/shard_map/while/body/eval_jaxpr/ijh,ihp->jhp/dot_general | solution.py:49
  373.8 6.9 %multiply_reduce_fusion.8 = (f32[256,32]{0,1:T(8,128)S(1)}, f32[256,32]{0,1:T(8,128)S(1)}, f32[256,256]{0,1:T(8,128)S(1)}) fusion(f32[256,256]{0,1:T(8,128)S(1)} %fusion.217, f32[256,32]{0,1:T(8,128)S(1)} %fusion.216, pred[256,256]{0,1:T(8,128)(4,1)S(1)} %iota_compare_fusion.3, f32[256,32]{0,1:T(8,128)S(1)} %dynamic-slice_bitcast_fusion.7, ...), kind=kOutput, calls=%fused_computation.39.clone.1.clone | convolution fusion | flops 287227904 | bytes 2851840 | tf_op jit(solution)/shard_map/while/body/eval_jaxpr/ihp,jhp->ijh/dot_general | solution.py:43
  392.8 5.0 fusion.219
  410.3 8.6 %fusion.218 = (f32[256,32]{0,1:T(8,128)S(1)}, f32[256,32]{0,1:T(8,128)S(1)}, bf16[256,32,64]{0,2,1:T(8,128)(2,1)S(1)}) fusion(f32[256,32,64]{0,2,1:T(8,128)S(1)} %fusion.215, f32[256,32]{0,1:T(8,128)S(1)} %dynamic-slice_bitcast_fusion.7, bf16[4,256,32,64]{1,3,2,0:T(8,128)(2,1)} %get-tuple-element.1292, s32[]{:T(128)} %get-tuple-element.1260, ...), kind=kOutput, calls=%fused_computation.56.clone.1.clone | convolution fusion | flops 1625800704 | bytes 6817280 | tf_op jit(solution)/shard_map/while/body/eval_jaxpr/ijh,ihp->jhp/dot_general | solution.py:49
  418.9 6.9 %multiply_reduce_fusion.8 = (f32[256,32]{0,1:T(8,128)S(1)}, f32[256,32]{0,1:T(8,128)S(1)}, f32[256,256]{0,1:T(8,128)S(1)}) fusion(f32[256,256]{0,1:T(8,128)S(1)} %fusion.217, f32[256,32]{0,1:T(8,128)S(1)} %fusion.216, pred[256,256]{0,1:T(8,128)(4,1)S(1)} %iota_compare_fusion.3, f32[256,32]{0,1:T(8,128)S(1)} %dynamic-slice_bitcast_fusion.7, ...), kind=kOutput, calls=%fused_computation.39.clone.1.clone | convolution fusion | flops 287227904 | bytes 2851840 | tf_op jit(solution)/shard_map/while/body/eval_jaxpr/ihp,jhp->ijh/dot_general | solution.py:43
  455.4 8.6 %fusion.218 = (f32[256,32]{0,1:T(8,128)S(1)}, f32[256,32]{0,1:T(8,128)S(1)}, bf16[256,32,64]{0,2,1:T(8,128)(2,1)S(1)}) fusion(f32[256,32,64]{0,2,1:T(8,128)S(1)} %fusion.215, f32[256,32]{0,1:T(8,128)S(1)} %dynamic-slice_bitcast_fusion.7, bf16[4,256,32,64]{1,3,2,0:T(8,128)(2,1)} %get-tuple-element.1292, s32[]{:T(128)} %get-tuple-element.1260, ...), kind=kOutput, calls=%fused_computation.56.clone.1.clone | convolution fusion | flops 1625800704 | bytes 6817280 | tf_op jit(solution)/shard_map/while/body/eval_jaxpr/ijh,ihp->jhp/dot_general | solution.py:49
  464.2 6.9 %multiply_reduce_fusion.8 = (f32[256,32]{0,1:T(8,128)S(1)}, f32[256,32]{0,1:T(8,128)S(1)}, f32[256,256]{0,1:T(8,128)S(1)}) fusion(f32[256,256]{0,1:T(8,128)S(1)} %fusion.217, f32[256,32]{0,1:T(8,128)S(1)} %fusion.216, pred[256,256]{0,1:T(8,128)(4,1)S(1)} %iota_compare_fusion.3, f32[256,32]{0,1:T(8,128)S(1)} %dynamic-slice_bitcast_fusion.7, ...), kind=kOutput, calls=%fused_computation.39.clone.1.clone | convolution fusion | flops 287227904 | bytes 2851840 | tf_op jit(solution)/shard_map/while/body/eval_jaxpr/ihp,jhp->ijh/dot_general | solution.py:43
  500.7 8.5 %fusion.218 = (f32[256,32]{0,1:T(8,128)S(1)}, f32[256,32]{0,1:T(8,128)S(1)}, bf16[256,32,64]{0,2,1:T(8,128)(2,1)S(1)}) fusion(f32[256,32,64]{0,2,1:T(8,128)S(1)} %fusion.215, f32[256,32]{0,1:T(8,128)S(1)} %dynamic-slice_bitcast_fusion.7, bf16[4,256,32,64]{1,3,2,0:T(8,128)(2,1)} %get-tuple-element.1292, s32[]{:T(128)} %get-tuple-element.1260, ...), kind=kOutput, calls=%fused_computation.56.clone.1.clone | convolution fusion | flops 1625800704 | bytes 6817280 | tf_op jit(solution)/shard_map/while/body/eval_jaxpr/ijh,ihp->jhp/dot_general | solution.py:49
  509.3 6.9 %multiply_reduce_fusion.8 = (f32[256,32]{0,1:T(8,128)S(1)}, f32[256,32]{0,1:T(8,128)S(1)}, f32[256,256]{0,1:T(8,128)S(1)}) fusion(f32[256,256]{0,1:T(8,128)S(1)} %fusion.217, f32[256,32]{0,1:T(8,128)S(1)} %fusion.216, pred[256,256]{0,1:T(8,128)(4,1)S(1)} %iota_compare_fusion.3, f32[256,32]{0,1:T(8,128)S(1)} %dynamic-slice_bitcast_fusion.7, ...), kind=kOutput, calls=%fused_computation.39.clone.1.clone | convolution fusion | flops 287227904 | bytes 2851840 | tf_op jit(solution)/shard_map/while/body/eval_jaxpr/ihp,jhp->ijh/dot_general | solution.py:43
  528.3 5.0 fusion.219
  544.4 64.0 %psum.23 = f32[3,32]{1,0:T(4,128)S(1)} all-reduce(f32[3,32]{1,0:T(4,128)S(1)} %pad_maximum_fusion.2), channel_id=1, replica_groups=mesh['seq'=16,'head'=4,'dp'=2] {'seq','dp'}, use_global_device_ids=true, to_apply=%region_26.27 | all-reduce | flops 96 | bytes 768 | tf_op jit(solution)/shard_map/psum | solution.py:163
  (318 shorter events, 221.1 us)
Async XLA Ops:
  7.2 210.6 %all-gather.6.cloned.1.call-start = ((), (), s32[]{:S(2)}) async-start(), calls=%async_computation.1 | async-start | bytes 17825792 | tf_op jit(solution)/shard_map/all_gather | solution.py:16
  8.2 22.1 %copy-start.2 = (f32[4,256,32]{1,0,2:T(4,128)}, f32[4,256,32]{1,0,2:T(4,128)S(1)}, u32[]{:S(2)}) copy-start(f32[4,256,32]{1,0,2:T(4,128)S(1)} %squeeze.143) | copy-start | bytes 393220
  9.8 20.5 %copy-start.3 = (f32[4,256,32]{1,0,2:T(4,128)}, f32[4,256,32]{1,0,2:T(4,128)S(1)}, u32[]{:S(2)}) copy-start(f32[4,256,32]{1,0,2:T(4,128)S(1)} %get-tuple-element.813) | copy-start | bytes 393220
  100.3 6.2 %copy-start.7 = (u32[128]{0:T(128)S(1)}, u32[128]{0:T(128)}, u32[]{:S(2)}) copy-start(u32[128]{0:T(128)} %constant.196) | copy-start | bytes 1540
  105.6 221.5 %all-gather.4.cloned.1.call-start = ((), (), s32[]{:S(2)}) async-start(), calls=%async_computation | async-start | bytes 17825792 | tf_op jit(solution)/shard_map/all_gather | solution.py:16
  106.4 504.3 %all-reduce.4.cloned.1.call-start = ((), (), s32[]{:S(2)}) async-start(), calls=%async_computation.2 | async-start | bytes 2097152 | tf_op jit(solution)/shard_map/psum | solution.py:147
  357.2 2.4 copy-start.5
  359.7 183.3 %copy-start.4 = (f32[32]{0:T(128)S(1)}, f32[32]{0:T(128)}, u32[]{:S(2)}) copy-start(f32[32]{0:T(128)} %param.22) | copy-start | bytes 388
  359.7 184.7 %copy-start.6 = (f32[32]{0:T(128)S(1)}, f32[32]{0:T(128)}, u32[]{:S(2)}) copy-start(f32[32]{0:T(128)} %param.21) | copy-start | bytes 388
  359.7 5.2 copy-start
  391.8 13.3 %copy-start.1 = (f32[4,256,32]{1,2,0:T(8,128)S(1)}, f32[4,256,32]{1,2,0:T(8,128)}, u32[]{:S(2)}) copy-start(f32[4,256,32]{1,2,0:T(8,128)} %copy-done) | copy-start | bytes 393220 | tf_op jit(solution)/shard_map/while
  405.1 5.1 copy-start
  436.9 13.3 %copy-start.1 = (f32[4,256,32]{1,2,0:T(8,128)S(1)}, f32[4,256,32]{1,2,0:T(8,128)}, u32[]{:S(2)}) copy-start(f32[4,256,32]{1,2,0:T(8,128)} %copy-done) | copy-start | bytes 393220 | tf_op jit(solution)/shard_map/while
  450.3 5.1 copy-start
  482.1 13.4 %copy-start.1 = (f32[4,256,32]{1,2,0:T(8,128)S(1)}, f32[4,256,32]{1,2,0:T(8,128)}, u32[]{:S(2)}) copy-start(f32[4,256,32]{1,2,0:T(8,128)} %copy-done) | copy-start | bytes 393220 | tf_op jit(solution)/shard_map/while
  495.5 5.1 copy-start
  527.3 13.4 %copy-start.1 = (f32[4,256,32]{1,2,0:T(8,128)S(1)}, f32[4,256,32]{1,2,0:T(8,128)}, u32[]{:S(2)}) copy-start(f32[4,256,32]{1,2,0:T(8,128)} %copy-done) | copy-start | bytes 393220 | tf_op jit(solution)/shard_map/while
Sparse Core Ops, SparseCore 0:
  105.7 111.9 all-gather.5
  220.2 106.8 all-gather.3
  541.8 43.9 all-reduce.3
where the time goes:
time: 624 us; the launch traced here: 619 us
  matrix products  173 us (28%)
  waiting for transfers between devices  151 us (24%)
  blocking collectives  103 us (17%)
  other arithmetic  91 us (15%)
  local copies, waits for them, and re-layouts  85 us (14%)
  between operations  14.6 us (2%)
    all_gather x2, waiting for transfers between devices, carried_in(): everything = jax.tree.map(lambda part: lax.all_gather(part, axis), array)  150 us
    psum x1, blocking collectives, shards(): lax.psum(jnp.stack([d_alog, d_bias, d_skip]), ('seq', 'dp')) * scale  64 us
    select_n x32, other arithmetic, hop(): return jax.tree.map(lambda a, b: jnp.where(reached, a, b), new, before)  47.1 us
    unnamed x1, blocking collectives  38.7 us
    dot_general x4, matrix products, block_grads(): jnp.einsum('ijh,ihp->jhp', weight, yf, precision=HIGH)  34.6 us
    dot_general x4, matrix products, block_grads(): jnp.einsum('ihp,jhp->ijh', y_half, x_half, preferred_element_type=jnp.flo...  27.4 us
    dynamic_update_slice x24, local copies, waits for them, and re-layouts, shards(): lax.map(full_terms, (x_blocks, y_blocks, b_half, c_half, b_blocks, c_bloc...  20.6 us
    dot_general x4, matrix products, block_grads(): jnp.einsum('jhp,hpn->jn', xs * wend[:, :, None], gout, precision=HIGH)  20 us
  transfers between devices with their start and end apart: 3, of which 2 were waited for; matrix products, arithmetic and copies ran while one was open for 6% of the time, Pallas kernels for 0%

commit v1 on v0

v1 whole, which is shorter than its diff:
```python
import functools
import math

import jax
import jax.numpy as jnp
from jax import lax
from jax.experimental import pallas as pl
from jax.experimental.pallas import tpu as pltpu
from jax.sharding import PartitionSpec as P

Q = 64
CHUNK = 256
HEADDIM = 64
LANES = 128
HIGH = lax.Precision.HIGHEST
F32 = jnp.float32
BF16 = jnp.bfloat16
VMEM_LIMIT = 56 * 1024 * 1024


def dot_nn(a, b, precision=None):
    return lax.dot_general(a, b, (((1,), (0,)), ((), ())), precision=precision, preferred_element_type=F32)


def dot_nt(a, b):
    return lax.dot_general(a, b, (((1,), (1,)), ((), ())), preferred_element_type=F32)


def halves(value):
    hi = value.astype(BF16)
    return hi, (value - hi.astype(F32)).astype(BF16)


def iota(shape, dim):
    return lax.broadcasted_iota(jnp.int32, shape, dim)


def triangle(upper):
    r, c = iota((Q, Q), 0), iota((Q, Q), 1)
    return jnp.where(r <= c if upper else r >= c, 1.0, 0.0).astype(F32)


def repeat_heads(value, heads):
    pick = jnp.where(iota((heads, LANES), 1) % heads == iota((heads, LANES), 0), 1.0, 0.0)
    return dot_nn(value, pick.astype(F32), HIGH)


def packed(value, heads, terms):
    lane = iota(value.shape, 1)
    total = jnp.zeros_like(value)
    rest = value
    for term in range(terms):
        part = rest.astype(BF16).astype(F32)
        total = jnp.where((lane >= term * heads) & (lane < (term + 1) * heads), part, total)
        rest = rest - part
    return total.astype(BF16)


def head_lanes(heads, width):
    shape = (LANES, width)
    return jnp.where(iota(shape, 0) % heads == iota(shape, 1) // HEADDIM, 1.0, 0.0).astype(BF16)


def edges_kernel(heads, x_ref, y_ref, bc_ref, dt_ref, bias_ref, alog_ref, ends_ref, starts_ref, decay_ref,
                 pe, pf, bt, ct, sel, xs, ys, dec):
    length = dt_ref.shape[0]
    blocks = length // Q
    step = pl.program_id(0)

    @pl.when(step == 0)
    def _():
        sel[...] = head_lanes(heads, sel.shape[1])
        rate = -jnp.exp(repeat_heads(jnp.broadcast_to(alog_ref[...], (8, heads)), heads))[:1]
        dt = jax.nn.softplus(repeat_heads(dt_ref[...] + bias_ref[...], heads))
        tri = triangle(False)
        cums = [dot_nn(tri, dt[k * Q:(k + 1) * Q] * rate, HIGH) for k in range(blocks)]
        before = jnp.zeros((1, LANES), F32)
        for k in range(blocks):
            pe[pl.ds(k * Q, Q), :] = packed(jnp.exp(cums[k] + before), heads, 2)
            before = before + cums[k][Q - 1:Q]
        after = jnp.zeros((1, LANES), F32)
        for k in reversed(range(blocks)):
            last = cums[k][Q - 1:Q]
            pf[pl.ds(k * Q, Q), :] = packed(dt[k * Q:(k + 1) * Q] * jnp.exp((last - cums[k]) + after), heads, 2)
            after = after + last
        dec[...] = packed(jnp.broadcast_to(jnp.exp(before), (8, LANES)), heads, 3)
        b_t = jnp.transpose(bc_ref[:, :LANES].astype(F32)).astype(BF16)
        c_t = jnp.transpose(bc_ref[:, LANES:].astype(F32)).astype(BF16)
        bt[:, :length] = b_t
        bt[:, length:] = b_t
        ct[:, :length] = c_t
        ct[:, length:] = c_t

    here = sel[:, pl.ds(pl.multiple_of(step * CHUNK, CHUNK), CHUNK)]
    hi, lo = halves(dot_nn(pf[...], here) * x_ref[...].astype(F32))
    xs[:length] = hi
    xs[length:] = lo
    ends_ref[...] = dot_nn(bt[...], xs[...])
    hi, lo = halves(dot_nn(pe[...], here) * y_ref[...].astype(F32))
    ys[:length] = hi
    ys[length:] = lo
    starts_ref[...] = dot_nn(ct[...], ys[...])
    decay_ref[...] = dot_nn(dec[...], here)


def edges(x, y, bc, dt, bias, alog):
    length, width = x.shape
    heads = dt.shape[1]
    state = bc.shape[1] // 2
    whole = pl.BlockSpec(memory_space=pltpu.VMEM)
    piece = lambda rows: pl.BlockSpec((rows, CHUNK), lambda i: (0, i))
    return pl.pallas_call(
        functools.partial(edges_kernel, heads),
        grid=(width // CHUNK,),
        out_shape=(
            jax.ShapeDtypeStruct((state, width), F32),
            jax.ShapeDtypeStruct((state, width), F32),
            jax.ShapeDtypeStruct((8, width), F32),
        ),
        in_specs=[piece(length), piece(length), whole, whole, whole, whole],
        out_specs=(piece(state), piece(state), piece(8)),
        scratch_shapes=[
            pltpu.VMEM((length, LANES), BF16),
            pltpu.VMEM((length, LANES), BF16),
            pltpu.VMEM((state, 2 * length), BF16),
            pltpu.VMEM((state, 2 * length), BF16),
            pltpu.VMEM((LANES, width), BF16),
            pltpu.VMEM((2 * length, CHUNK), BF16),
            pltpu.VMEM((2 * length, CHUNK), BF16),
            pltpu.VMEM((8, LANES), BF16),
        ],
        compiler_params=pltpu.CompilerParams(vmem_limit_bytes=VMEM_LIMIT, dimension_semantics=("arbitrary",)),
        cost_estimate=pl.CostEstimate(flops=8 * length * width * state, bytes_accessed=4 * length * width, transcendentals=0),
    )(x, y, bc, dt, bias, alog)


def main_kernel(heads, xf_ref, yf_ref, xb_ref, yb_ref, bc_ref, dt_ref, bias_ref, alog_ref, skip_ref, hin_ref, gin_ref,
                gx_ref, gbc_ref, gdt_ref, gheads_ref,
                pe, pf, dts, shs, sel, rows, vs, ws, zf, zb, ll, xx, prods, hst, gst, yx):
    length = dt_ref.shape[0]
    width = sel.shape[1]
    blocks = length // Q
    step = pl.program_id(0)
    kf = step
    kb = blocks - 1 - step
    chunks = [slice(c * CHUNK, (c + 1) * CHUNK) for c in range(width // CHUNK)]
    rate = -jnp.exp(repeat_heads(jnp.broadcast_to(alog_ref[...], (8, heads)), heads))[:1]

    @pl.when(step == 0)
    def _():
        sel[...] = head_lanes(heads, width)
        shifted = repeat_heads(dt_ref[...] + bias_ref[...], heads)
        shs[...] = shifted
        dt = jax.nn.softplus(shifted)
        dts[...] = dt
        tri = triangle(False)
        mids, lasts = [], []
        for k in range(blocks):
            here = dt[k * Q:(k + 1) * Q]
            cum = dot_nn(tri, here * rate, HIGH)
            mid = cum[Q // 2 - 1:Q // 2]
            pe[pl.ds(k * Q, Q), :] = packed(jnp.exp(cum - mid), heads, 2)
            pf[pl.ds(k * Q, Q), :] = packed(here * jnp.exp(mid - cum), heads, 2)
            mids.append(mid)
            lasts.append(cum[Q - 1:Q])
        for k in range(blocks):
            gone = jnp.broadcast_to(jnp.exp(lasts[k] - mids[k]), (8, LANES))
            come = jnp.broadcast_to(jnp.exp(mids[k]), (8, LANES))
            factor = packed(jnp.where(iota((8, LANES), 0) == 0, gone, come), heads, 3)
            rows[k] = dot_nn(factor, sel[...])
        skips = repeat_heads(jnp.broadcast_to(skip_ref[...], (8, heads)), heads)
        rows[blocks] = dot_nn(packed(skips, heads, 3), sel[...])
        yx[...] = jnp.zeros_like(yx)
        gbc_ref[...] = jnp.zeros_like(gbc_ref)
        for c in chunks:
            h = hin_ref[:, c] * rows[0, 1:2, c]
            hst[:, c] = h
            zf[0:128, c], zf[256:384, c] = halves(h)
            g = gin_ref[:, c] * rows[blocks - 1, 0:1, c]
            gst[:, c] = g
            zb[0:128, c], zb[256:384, c] = halves(g)

    spanf = pl.ds(pl.multiple_of(kf * Q, Q), Q)
    spanb = pl.ds(pl.multiple_of(kb * Q, Q), Q)
    lane = iota((Q, 2 * Q), 1)
    row = iota((Q, 2 * Q), 0)

    b_f, c_f = bc_ref[spanf, :LANES], bc_ref[spanf, LANES:]
    b_b, c_b = bc_ref[spanb, :LANES], bc_ref[spanb, LANES:]
    b_ff = jnp.concatenate([b_f, b_f], axis=0)
    c_bb = jnp.concatenate([c_b, c_b], axis=0)
    zero = jnp.zeros((Q, 2 * Q), F32)

    lower = row >= lane % Q
    s_hi, s_lo = halves(jnp.where(lower, dot_nt(c_f, b_ff), zero))
    first_f = jnp.concatenate([c_f, s_hi], axis=1)
    second_f = jnp.concatenate([s_lo, c_f], axis=1)
    upper = row <= lane % Q
    s_hi, s_lo = halves(jnp.where(upper, dot_nt(b_b, c_bb), zero))
    first_b = jnp.concatenate([b_b, s_hi], axis=1)
    second_b = jnp.concatenate([s_lo, b_b], axis=1)

    for c in chunks:
        e = dot_nn(pe[spanf, :], sel[:, c])
        f = dot_nn(pf[spanf, :], sel[:, c])
        lifted = e * yf_ref[:, c].astype(F32)
        xs = f * xf_ref[:, c].astype(F32)
        zf[192:256, c], zf[128:192, c] = halves(xs)
        ll[0:64, c], ll[64:128, c] = halves(lifted)
        out = dot_nn(first_f, zf[0:256, c]) + dot_nn(second_f, zf[128:384, c])
        prods[0:64, c], prods[64:128, c] = halves(lifted * out)

        e = dot_nn(pe[spanb, :], sel[:, c])
        f = dot_nn(pf[spanb, :], sel[:, c])
        y = yb_ref[:, c].astype(F32)
        x = xb_ref[:, c].astype(F32)
        lifted = e * y
        xs = f * x
        zb[192:256, c], zb[128:192, c] = halves(lifted)
        xx[0:64, c], xx[64:128, c] = halves(xs)
        out = dot_nn(first_b, zb[0:256, c]) + dot_nn(second_b, zb[128:384, c])
        prods[128:192, c], prods[192:256, c] = halves(xs * out)
        gx_ref[:, c] = (f * out + rows[blocks, :1, c] * y).astype(BF16)
        yx[:, c] += jnp.sum((y * x).reshape(Q // 8, 8, CHUNK), axis=0)

    sums = dot_nt(prods[...], sel[...])
    vs[spanf, :] = sums[0:64] + sums[64:128]
    ws[spanb, :] = sums[128:192] + sums[192:256]

    r1 = dot_nt(ll[...], zf[0:256, :])
    r2 = dot_nt(ll[0:64, :], zf[256:384, :])
    pair = r1[:64, 128:] + r1[64:, 128:]
    pair = jnp.where(lower, pair, zero)
    p_hi, p_lo = halves(pair)
    grad_c = r1[:64, :128] + r1[64:, :128] + r2 + dot_nn(p_hi, b_ff) + dot_nn(p_lo, b_ff)
    turned = jnp.transpose(pair)
    t_hi, t_lo = halves(turned[:64] + turned[64:])
    gbc_ref[spanf, LANES:] = grad_c
    gbc_ref[spanf, :LANES] += dot_nn(t_hi, c_f) + dot_nn(t_lo, c_f)
    r1 = dot_nt(xx[...], zb[0:128, :])
    r2 = dot_nt(xx[0:64, :], zb[256:384, :])
    gbc_ref[spanb, :LANES] += r1[:64] + r1[64:] + r2

    bt = jnp.transpose(b_ff.astype(F32)).astype(BF16)
    ct = jnp.transpose(c_bb.astype(F32)).astype(BF16)
    last = step == blocks - 1
    for c in chunks:
        come = jnp.where(last, 1.0, rows[jnp.minimum(kf + 1, blocks - 1), 1:2, c])
        h = (hst[:, c] + dot_nn(bt, zf[128:256, c])) * rows[kf, 0:1, c] * come
        hst[:, c] = h
        zf[0:128, c], zf[256:384, c] = halves(h)
        g = (gst[:, c] + dot_nn(ct, zb[128:256, c])) * rows[kb, 1:2, c] * rows[jnp.maximum(kb - 1, 0), 0:1, c]
        gst[:, c] = g
        zb[0:128, c], zb[256:384, c] = halves(g)

    @pl.when(step == blocks - 1)
    def _():
        closing = jnp.sum(gin_ref[...] * hst[...], axis=0, keepdims=True)
        totals = jnp.concatenate([closing, jnp.sum(yx[...], axis=0, keepdims=True), jnp.zeros((14, width), F32)], axis=0)
        hi, lo = halves(totals)
        totals = dot_nt(hi, sel[...]) + dot_nt(lo, sel[...])
        after = totals[0:1]
        tri = triangle(True)
        d_alog = jnp.zeros((1, LANES), F32)
        d_bias = jnp.zeros((1, LANES), F32)
        for k in reversed(range(blocks)):
            span = slice(k * Q, (k + 1) * Q)
            w = ws[span]
            dt = dts[span]
            dlog = dot_nn(tri, vs[span] - w, HIGH) + after
            after = dlog[0:1]
            grad_dt = (w / dt + dlog * rate) * jax.nn.sigmoid(shs[span])
            gdt_ref[span, :] = grad_dt[:, :heads]
            d_alog = d_alog + jnp.sum(dlog * dt, axis=0, keepdims=True)
            d_bias = d_bias + jnp.sum(grad_dt, axis=0, keepdims=True)
        gheads_ref[...] = jnp.concatenate(
            [d_alog * rate, d_bias, totals[1:2], jnp.zeros((5, LANES), F32)], axis=0)


def main(x, y, bc, dt, bias, alog, skip, hin, gin):
    length, width = x.shape
    heads = dt.shape[1]
    state = bc.shape[1] // 2
    blocks = length // Q
    whole = pl.BlockSpec(memory_space=pltpu.VMEM)
    ahead = pl.BlockSpec((Q, width), lambda i: (i, 0))
    back = pl.BlockSpec((Q, width), lambda i: (blocks - 1 - i, 0))
    return pl.pallas_call(
        functools.partial(main_kernel, heads),
        grid=(blocks,),
        out_shape=(
            jax.ShapeDtypeStruct((length, width), BF16),
            jax.ShapeDtypeStruct((length, 2 * state), F32),
            jax.ShapeDtypeStruct((length, heads), F32),
            jax.ShapeDtypeStruct((8, LANES), F32),
        ),
        in_specs=[ahead, ahead, back, back] + [whole] * 7,
        out_specs=(back, whole, whole, whole),
        scratch_shapes=[
            pltpu.VMEM((length, LANES), BF16),
            pltpu.VMEM((length, LANES), BF16),
            pltpu.VMEM((length, LANES), F32),
            pltpu.VMEM((length, LANES), F32),
            pltpu.VMEM((LANES, width), BF16),
            pltpu.VMEM((blocks + 1, 8, width), F32),
            pltpu.VMEM((length, LANES), F32),
            pltpu.VMEM((length, LANES), F32),
            pltpu.VMEM((384, width), BF16),
            pltpu.VMEM((384, width), BF16),
            pltpu.VMEM((128, width), BF16),
            pltpu.VMEM((128, width), BF16),
            pltpu.VMEM((256, width), BF16),
            pltpu.VMEM((state, width), F32),
            pltpu.VMEM((state, width), F32),
            pltpu.VMEM((8, width), F32),
        ],
        compiler_params=pltpu.CompilerParams(vmem_limit_bytes=VMEM_LIMIT, dimension_semantics=("arbitrary",)),
        cost_estimate=pl.CostEstimate(flops=60 * length * width * state, bytes_accessed=12 * length * width, transcendentals=0),
    )(x, y, x, y, bc, dt, bias, alog, skip, hin, gin)


def carried_in(decay, value, axis, reverse):
    count, place = (lax.axis_size(axis), lax.axis_index(axis))
    decays = lax.all_gather(decay, axis)
    values = lax.all_gather(value, axis)

    def hop(k, before):
        at = count - 1 - k if reverse else k
        reached = at > place if reverse else at < place
        return jnp.where(reached, decays[at] * before + values[at], before)

    return lax.fori_loop(0, count, hop, jnp.zeros_like(value))


def shards(inputs_x, inputs_bc, dt_raw, grad_out, a_log, dt_bias, skip):
    length = inputs_x.shape[1]
    heads = a_log.shape[0]
    x, y, bc, dt = inputs_x[0], grad_out[0], inputs_bc[0], dt_raw[0]
    bias, alog, skips = dt_bias[None], a_log[None], skip[None]
    ends, starts, decay = edges(x, y, bc, dt, bias, alog)
    hin = carried_in(decay[:1], ends, "seq", False)
    gin = carried_in(decay[:1], starts, "seq", True)
    grad_x, grad_bc, grad_dt, sums = main(x, y, bc, dt, bias, alog, skips, hin, gin)
    grad_bc = lax.psum(grad_bc, "head")
    sequences = inputs_x.shape[0] * lax.axis_size("dp")
    scale = 1.0 / math.sqrt(sequences * length * lax.axis_size("seq"))
    grad_heads = lax.psum(sums[:3, :heads], ("seq", "dp")) * scale
    return (grad_x[None], grad_bc[None], grad_dt[None], grad_heads)


def solution(mesh):
    placed = (
        P("dp", "seq", "head"),
        P("dp", "seq", None),
        P("dp", "seq", "head"),
        P("dp", "seq", "head"),
        P("head"),
        P("head"),
        P("head"),
    )
    return jax.shard_map(
        shards,
        mesh=mesh,
        in_specs=placed,
        out_specs=(
            P("dp", "seq", "head"),
            P("dp", "seq", None),
            P("dp", "seq", "head"),
            P(None, "head"),
        ),
        check_vma=False,
    )
```

time: 624 us -> 429 us (0.69)
  matrix products: 173 us -> 0 us
  Pallas kernels: 0 us -> 85.7 us
  local copies, waits for them, and re-layouts: 85 us -> 7.81 us
  other arithmetic: 91 us -> 69.2 us
  blocking collectives: 103 us -> 89.4 us
  waiting for transfers between devices: 151 us -> 161 us
    dot_general x44 -> x0, matrix products: 173 us -> none  [the longest x4 34.6 us: block_grads(): jnp.einsum('ijh,ihp->jhp', weight, yf, precision=HIGH)]
    pallas_call x0 -> x2, Pallas kernels: none -> 85.7 us  [the longest x1 72.5 us: main(): pl.pallas_call(functools.partial(main_kernel, heads), grid=(blocks,), out...]
    unnamed x1 -> x0, blocking collectives: 38.7 us -> none
    another operation x20 -> x0, local copies, waits for them, and re-layouts: 27 us -> none  [the longest x1 12.9 us: shards(): x_blocks = inputs_x[0].reshape(blocks, GROUP, heads, headdim)]
    all_gather x0 -> x1, blocking collectives: none -> 25.4 us  [carried_in(): decays = lax.all_gather(decay, axis)]
    select_n x32, other arithmetic: 47.1 us -> 68.6 us  [hop(): return jnp.where(reached, decays[at] * before + values[at], before)]
    while x19 -> x0, local copies, waits for them, and re-layouts: 21.4 us -> none  [the longest x2 11 us: shards(): lax.map(local_terms, (x_blocks, y_blocks, b_blocks, c_blocks, dt_blocks,...]
    dynamic_update_slice x24 -> x0, local copies, waits for them, and re-layouts: 20.6 us -> none  [shards(): lax.map(full_terms, (x_blocks, y_blocks, b_half, c_half, b_blocks, c_bloc...]
  transfers between devices with their start and end apart: 3 -> 3, of which waited for: 2 -> 2; matrix products, arithmetic and copies ran while one was open for 6% -> 9% of each run, Pallas kernels for 0% -> 0%
where the time goes in v1:
time: 429 us; the launch traced here: 428 us
  waiting for transfers between devices  161 us (38%)
  blocking collectives  89.4 us (21%)
  Pallas kernels  85.7 us (20%)
  other arithmetic  69.2 us (16%)
  between operations  13.8 us (3%)
  local copies, waits for them, and re-layouts  7.81 us (2%)
    all_gather x2, waiting for transfers between devices, carried_in(): values = lax.all_gather(value, axis)  160 us
    pallas_call x1, Pallas kernels, main(): pl.pallas_call(functools.partial(main_kernel, heads), grid=(blocks,), out...  72.5 us
    select_n x32, other arithmetic, hop(): return jnp.where(reached, decays[at] * before + values[at], before)  68.6 us
    psum x1, blocking collectives, shards(): grad_heads = lax.psum(sums[:3, :heads], ('seq', 'dp')) * scale  63.9 us
    all_gather x1, blocking collectives, carried_in(): decays = lax.all_gather(decay, axis)  25.4 us
    pallas_call x1, Pallas kernels, edges(): pl.pallas_call(functools.partial(edges_kernel, heads), grid=(width // CHU...  13.2 us
  transfers between devices with their start and end apart: 3, of which 2 were waited for; matrix products, arithmetic and copies ran while one was open for 9% of the time, Pallas kernels for 0%

profile of v1, /device:TPU:0, one launch (start us, length us, event | category | flops | bytes accessed | tf_op | source)
XLA Modules:
  0.0 427.7 jit_solution(8127581867457870837)
XLA Ops:
  9.1 13.2 %shard_map.102 = (f32[128,2048]{1,0:T(8,128)}, f32[128,2048]{1,0:T(8,128)}, f32[8,2048]{1,0:T(8,128)}) custom-call(bf16[1024,2048]{1,0:T(8,128)(2,1)} %bitcast.32, bf16[1024,2048]{1,0:T(8,128)(2,1)} %bitcast.35, bf16[1024,256]{1,0:T(8,128)(2,1)} %bitcast.45, f32[1024,32]{1,0:T(8,128)} %bitcast.38, f32[1,32]{1,0:T(1,128)} %bitcast.48, f32[1,32]{1,0:T(1,128)} %bitcast.50), custom_call_target="tpu_custom_call" | custom-call | flops 2147483648 | bytes 8388608 | tf_op jit(solution)/shard_map/pallas_call | solution.py:112
  24.0 25.4 %all-gather.3 = f32[16,1,2048]{2,1,0:T(1,128)S(1)} all-gather(f32[1,1,2048]{2,1,0:T(1,128)S(1)} %slice_bitcast_fusion), channel_id=2, replica_groups=mesh['seq'=16,'head'=4,'dp'=2] {'seq'}, dimensions={0}, use_global_device_ids=true | all-gather | bytes 139264 | tf_op jit(solution)/shard_map/all_gather | solution.py:324
  49.5 85.0 %all-gather.7.cloned.1.call-done = f32[2048,2048]{1,0:T(8,128)} async-done(((f32[128,2048]{1,0:T(8,128)}), f32[2048,2048]{1,0:T(8,128)}) %all-gather.7.cloned.1.call-update) | async-done | bytes 16777232 | tf_op jit(solution)/shard_map/all_gather | solution.py:325
  134.4 35.0 %while.30 = (s32[]{:T(128)}, f32[128,2048]{1,0:T(8,128)S(1)}, s32[]{:T(128)}, f32[16,1,2048]{2,1,0:T(1,128)S(1)}, f32[16,128,2048]{2,1,0:T(8,128)}, /*index=5*/s32[]{:T(128)}, s32[]{:T(128)}) while((s32[]{:T(128)}, f32[128,2048]{1,0:T(8,128)S(1)}, s32[]{:T(128)}, f32[16,1,2048]{2,1,0:T(1,128)S(1)}, f32[16,128,2048]{2,1,0:T(8,128)}, ...), condition=%wide.region_1.2_spmd.clone, body=%wide.region_0.1_spmd.clone.sunk | while | flops 1048580 | bytes 3170417 | solution.py:332
  143.1 2.1 fusion.4
  145.3 2.2 fusion.4
  156.3 2.2 fusion.4
  167.2 2.2 fusion.4
  169.4 75.0 %all-gather.9.cloned.1.call-done = f32[2048,2048]{1,0:T(8,128)} async-done(((f32[128,2048]{1,0:T(8,128)}), f32[2048,2048]{1,0:T(8,128)}) %all-gather.9.cloned.1.call-update) | async-done | bytes 16777232 | tf_op jit(solution)/shard_map/all_gather | solution.py:325
  244.4 34.9 %while.31 = (s32[]{:T(128)}, f32[128,2048]{1,0:T(8,128)S(1)}, s32[]{:T(128)}, f32[16,1,2048]{2,1,0:T(1,128)S(1)}, f32[16,128,2048]{2,1,0:T(8,128)}, /*index=5*/s32[]{:T(128)}, s32[]{:T(128)}, s32[]{:T(128)}, s32[]{:T(128)}) while((s32[]{:T(128)}, f32[128,2048]{1,0:T(8,128)S(1)}, s32[]{:T(128)}, f32[16,1,2048]{2,1,0:T(1,128)S(1)}, ...), condition=%wide.region_3.4_spmd.clone, body=%wide.region_2.3_spmd.clone.sunk | while | flops 1048584 | bytes 3170479 | solution.py:332
  246.6 2.1 fusion.5
  248.7 2.1 fusion.5
  250.9 2.1 fusion.5
  255.3 2.1 fusion.5
  257.5 2.1 fusion.5
  259.7 2.1 fusion.5
  261.9 2.1 fusion.5
  264.1 2.1 fusion.5
  266.2 2.1 fusion.5
  275.0 2.1 fusion.5
  277.2 2.1 fusion.5
  279.3 72.5 %shard_map.103 = (bf16[1024,2048]{1,0:T(8,128)(2,1)}, f32[1024,256]{1,0:T(8,128)}, f32[1024,32]{1,0:T(8,128)}, f32[8,128]{1,0:T(8,128)}) custom-call(bf16[1024,2048]{1,0:T(8,128)(2,1)} %bitcast.33, bf16[1024,2048]{1,0:T(8,128)(2,1)} %bitcast.36, bf16[1024,2048]{1,0:T(8,128)(2,1)} %bitcast.34, bf16[1024,2048]{1,0:T(8,128)(2,1)} %bitcast.37, ...), custom_call_target="tpu_custom_call" | custom-call | flops 16106127360 | bytes 25165824 | tf_op jit(solution)/shard_map/pallas_call | solution.py:288
  354.4 63.9 %psum.15 = f32[3,32]{1,0:T(4,128)S(1)} all-reduce(f32[3,32]{1,0:T(4,128)S(1)} %slice.8), channel_id=1, replica_groups=mesh['seq'=16,'head'=4,'dp'=2] {'seq','dp'}, use_global_device_ids=true, to_apply=%region_5.6 | all-reduce | flops 96 | bytes 768 | tf_op jit(solution)/shard_map/psum | solution.py:347
  418.9 2.3 copy.28
  (63 shorter events, 43.3 us)
Async XLA Ops:
  7.2 127.3 %all-gather.7.cloned.1.call-start = ((), (), s32[]{:S(2)}) async-start(), calls=%async_computation.1 | async-start | bytes 17825792 | tf_op jit(solution)/shard_map/all_gather | solution.py:325
  22.4 222.0 %all-gather.9.cloned.1.call-start = ((), (), s32[]{:S(2)}) async-start(), calls=%async_computation.2 | async-start | bytes 17825792 | tf_op jit(solution)/shard_map/all_gather | solution.py:325
  23.1 395.8 %all-reduce.2.cloned.1.call-start = ((), (), s32[]{:S(2)}) async-start(), calls=%async_computation | async-start | bytes 2097152 | tf_op jit(solution)/shard_map/psum | solution.py:344
Sparse Core Ops, SparseCore 0:
  22.5 111.9 all-gather.6
  137.5 106.8 all-gather.8
  351.9 43.9 all-reduce.1

commit v2 on v1

--- a/solution.py
+++ b/solution.py
@@ -61,95 +61,306 @@
     return jnp.where(iota(shape, 0) % heads == iota(shape, 1) // HEADDIM, 1.0, 0.0).astype(BF16)
 
 
-def edges_kernel(heads, x_ref, y_ref, bc_ref, dt_ref, bias_ref, alog_ref, ends_ref, starts_ref, decay_ref,
-                 pe, pf, bt, ct, sel, xs, ys, dec):
-    length = dt_ref.shape[0]
+def steps_of(dt_ref, bias_ref, heads):
+    turned = jnp.transpose(jnp.concatenate([dt_ref[...]] * (LANES // heads), axis=0))
+    return turned + repeat_heads(jnp.broadcast_to(bias_ref[...], (8, heads)), heads)[:1]
+
+
+def rates_of(alog_ref, heads):
+    return -jnp.exp(repeat_heads(jnp.broadcast_to(alog_ref[...], (8, heads)), heads))[:1]
+
+
+def edges_kernel(heads, x_ref, y_ref, bc_ref, dt_ref, bias_ref, alog_ref, hin_ref, gin_ref,
+                 pe, pf, bt, ct, sel, xb, yb, xs, ys, dec, mine, out0, got0, chip, gath, pre, inc, fin,
+                 load_sem, s0, r0, s1, r1, s2, r2, s3, r3):
+    length = bc_ref.shape[0]
     blocks = length // Q
-    step = pl.program_id(0)
-
-    @pl.when(step == 0)
-    def _():
-        sel[...] = head_lanes(heads, sel.shape[1])
-        rate = -jnp.exp(repeat_heads(jnp.broadcast_to(alog_ref[...], (8, heads)), heads))[:1]
-        dt = jax.nn.softplus(repeat_heads(dt_ref[...] + bias_ref[...], heads))
-        tri = triangle(False)
-        cums = [dot_nn(tri, dt[k * Q:(k + 1) * Q] * rate, HIGH) for k in range(blocks)]
-        before = jnp.zeros((1, LANES), F32)
-        for k in range(blocks):
-            pe[pl.ds(k * Q, Q), :] = packed(jnp.exp(cums[k] + before), heads, 2)
-            before = before + cums[k][Q - 1:Q]
-        after = jnp.zeros((1, LANES), F32)
-        for k in reversed(range(blocks)):
-            last = cums[k][Q - 1:Q]
-            pf[pl.ds(k * Q, Q), :] = packed(dt[k * Q:(k + 1) * Q] * jnp.exp((last - cums[k]) + after), heads, 2)
-            after = after + last
-        dec[...] = packed(jnp.broadcast_to(jnp.exp(before), (8, LANES)), heads, 3)
-        b_t = jnp.transpose(bc_ref[:, :LANES].astype(F32)).astype(BF16)
-        c_t = jnp.transpose(bc_ref[:, LANES:].astype(F32)).astype(BF16)
-        bt[:, :length] = b_t
-        bt[:, length:] = b_t
-        ct[:, :length] = c_t
-        ct[:, length:] = c_t
-
-    here = sel[:, pl.ds(pl.multiple_of(step * CHUNK, CHUNK), CHUNK)]
-    hi, lo = halves(dot_nn(pf[...], here) * x_ref[...].astype(F32))
-    xs[:length] = hi
-    xs[length:] = lo
-    ends_ref[...] = dot_nn(bt[...], xs[...])
-    hi, lo = halves(dot_nn(pe[...], here) * y_ref[...].astype(F32))
-    ys[:length] = hi
-    ys[length:] = lo
-    starts_ref[...] = dot_nn(ct[...], ys[...])
-    decay_ref[...] = dot_nn(dec[...], here)
+    groups = hin_ref.shape[0]
+    state = hin_ref.shape[1]
+    me = lax.axis_index("seq")
+    core = lax.rem(me, 2)
+    place = me // 2
+    ahead = core == 1
+    partner = me + 1 - 2 * core
+
+    def peer(d):
+        return lax.rem(place + d, groups)
+
+    def loads(i):
+        g = peer(1 + i)
+        span = pl.ds(pl.multiple_of(g * CHUNK, CHUNK), CHUNK)
+        return (pltpu.make_async_copy(x_ref.at[:, span], xb.at[i], load_sem.at[0, i]),
+                pltpu.make_async_copy(y_ref.at[:, span], yb.at[i], load_sem.at[1, i]))
+
+    def swap(i):
+        return pltpu.make_async_remote_copy(
+            src_ref=out0.at[i], dst_ref=got0.at[i], send_sem=s0.at[i], recv_sem=r0.at[i],
+            device_id={"seq": partner}, device_id_type=pl.DeviceIdType.MESH)
+
+    def spread(d):
+        return pltpu.make_async_remote_copy(
+            src_ref=chip.at[d - 1], dst_ref=gath.at[place], send_sem=s1.at[d - 1], recv_sem=r1.at[place],
+            device_id={"seq": peer(d) * 2 + core}, device_id_type=pl.DeviceIdType.MESH)
+
+    def spread_in(source):
+        return pltpu.make_async_remote_copy(
+            src_ref=chip.at[0], dst_ref=gath.at[source], send_sem=s1.at[0], recv_sem=r1.at[source],
+            device_id={"seq": source * 2 + core}, device_id_type=pl.DeviceIdType.MESH)
+
+    def back(pos):
+        return pltpu.make_async_remote_copy(
+            src_ref=pre.at[pos], dst_ref=inc.at[place], send_sem=s2.at[pos], recv_sem=r2.at[place],
+            device_id={"seq": pos * 2 + core}, device_id_type=pl.DeviceIdType.MESH)
+
+    def back_in(source):
+        return pltpu.make_async_remote_copy(
+            src_ref=pre.at[source], dst_ref=inc.at[source], send_sem=s2.at[source], recv_sem=r2.at[source],
+            device_id={"seq": source * 2 + core}, device_id_type=pl.DeviceIdType.MESH)
+
+    def hand(g):
+        return pltpu.make_async_remote_copy(
+            src_ref=inc.at[g], dst_ref=fin.at[g], send_sem=s3.at[g], recv_sem=r3.at[g],
+            device_id={"seq": partner}, device_id_type=pl.DeviceIdType.MESH)
+
+    for i in range(groups):
+        for copy in loads(i):
+            copy.start()
+    barrier = pltpu.get_barrier_semaphore()
+    pl.semaphore_signal(barrier, inc=1, device_id={"seq": partner}, device_id_type=pl.DeviceIdType.MESH)
+    for d in range(1, groups):
+        pl.semaphore_signal(barrier, inc=1, device_id={"seq": peer(d) * 2 + core}, device_id_type=pl.DeviceIdType.MESH)
+
+    sel[...] = head_lanes(heads, sel.shape[1])
+    rate = rates_of(alog_ref, heads)
+    dt = jax.nn.softplus(steps_of(dt_ref, bias_ref, heads))
+    tri = triangle(False)
+    cums = [dot_nn(tri, dt[k * Q:(k + 1) * Q] * rate, HIGH) for k in range(blocks)]
+    before = jnp.zeros((1, LANES), F32)
+    for k in range(blocks):
+        pe[pl.ds(k * Q, Q), :] = packed(jnp.exp(cums[k] + before), heads, 2)
+        before = before + cums[k][Q - 1:Q]
+    after = jnp.zeros((1, LANES), F32)
+    for k in reversed(range(blocks)):
+        last = cums[k][Q - 1:Q]
+        pf[pl.ds(k * Q, Q), :] = packed(dt[k * Q:(k + 1) * Q] * jnp.exp((last - cums[k]) + after), heads, 2)
+        after = after + last
+    dec[...] = packed(jnp.broadcast_to(jnp.exp(before), (8, LANES)), heads, 3)
+    b_t = jnp.transpose(bc_ref[:, :LANES].astype(F32)).astype(BF16)
+    c_t = jnp.transpose(bc_ref[:, LANES:].astype(F32)).astype(BF16)
+    bt[:, :length] = b_t
+    bt[:, length:] = b_t
+    ct[:, :length] = c_t
+    ct[:, length:] = c_t
+    pl.semaphore_wait(barrier, groups)
+
+    def combine(i):
+        swap(i).wait_recv()
+        keep = out0[i, state:state + 1, :]
+        value = mine[i] + keep * got0[i, :state, :]
+        decay = out0[i, state:, :] * got0[i, state:, :]
+        if i < groups - 1:
+            chip[i, :state, :] = value
+            chip[i, state:, :] = decay
+            spread(i + 1).start()
+        else:
+            gath[place, :state, :] = value
+            gath[place, state:, :] = decay
+
+    for i in range(groups):
+        g = peer(1 + i)
+        here = sel[:, pl.ds(pl.multiple_of(g * CHUNK, CHUNK), CHUNK)]
+        copy_x, copy_y = loads(i)
+        copy_x.wait()
+        hi, lo = halves(dot_nn(pf[...], here) * xb[i].astype(F32))
+        xs[:length] = hi
+        xs[length:] = lo
+        ends = dot_nn(bt[...], xs[...])
+        copy_y.wait()
+        hi, lo = halves(dot_nn(pe[...], here) * yb[i].astype(F32))
+        ys[:length] = hi
+        ys[length:] = lo
+        starts = dot_nn(ct[...], ys[...])
+        mine[i] = jnp.where(ahead, ends, starts)
+        out0[i, :state, :] = jnp.where(ahead, starts, ends)
+        out0[i, state:, :] = dot_nn(dec[...], here)
+        swap(i).start()
+        if i:
+            combine(i - 1)
+    combine(groups - 1)
+
+    total = jnp.zeros((state, CHUNK), F32)
+    for d in range(1, groups):
+        spread_in(peer(d)).wait_recv()
+    for k in range(groups):
+        pos = jnp.where(ahead, k, groups - 1 - k)
+
+        @pl.when(pos == place)
+        def _():
+            inc[place] = total
+
+        @pl.when(pos != place)
+        def _():
+            pre[pos] = total
+            back(pos).start()
+
+        total = gath[pos, state:state + 1, :] * total + gath[pos, :state, :]
+
+    for d in range(groups):
+        g = peer(d)
+        if d:
+            back_in(g).wait_recv()
+        hand(g).start()
+    for d in range(groups):
+        g = peer(d)
+        i = (d - 1) % groups
+        own = got0[i, state:state + 1, :] * inc[g] + got0[i, :state, :]
+        hand(g).wait_recv()
+        other = fin[g]
+        hin_ref[g] = jnp.where(ahead, own, other)
+        gin_ref[g] = jnp.where(ahead, other, own)
+    for i in range(groups):
+        swap(i).wait_send()
+        hand(i).wait_send()
+    for d in range(1, groups):
+        spread(d).wait_send()
+        back(peer(d)).wait_send()
 
 
 def edges(x, y, bc, dt, bias, alog):
     length, width = x.shape
-    heads = dt.shape[1]
+    heads = dt.shape[0]
     state = bc.shape[1] // 2
+    groups = width // CHUNK
     whole = pl.BlockSpec(memory_space=pltpu.VMEM)
-    piece = lambda rows: pl.BlockSpec((rows, CHUNK), lambda i: (0, i))
+    anywhere = pl.BlockSpec(memory_space=pl.ANY)
+    dma = pltpu.SemaphoreType.DMA
     return pl.pallas_call(
         functools.partial(edges_kernel, heads),
-        grid=(width // CHUNK,),
         out_shape=(
-            jax.ShapeDtypeStruct((state, width), F32),
-            jax.ShapeDtypeStruct((state, width), F32),
-            jax.ShapeDtypeStruct((8, width), F32),
+            jax.ShapeDtypeStruct((groups, state, CHUNK), F32),
+            jax.ShapeDtypeStruct((groups, state, CHUNK), F32),
         ),
-        in_specs=[piece(length), piece(length), whole, whole, whole, whole],
-        out_specs=(piece(state), piece(state), piece(8)),
+        in_specs=[anywhere, anywhere, whole, whole, whole, whole],
+        out_specs=(whole, whole),
         scratch_shapes=[
             pltpu.VMEM((length, LANES), BF16),
             pltpu.VMEM((length, LANES), BF16),
             pltpu.VMEM((state, 2 * length), BF16),
             pltpu.VMEM((state, 2 * length), BF16),
             pltpu.VMEM((LANES, width), BF16),
+            pltpu.VMEM((groups, length, CHUNK), BF16),
+            pltpu.VMEM((groups, length, CHUNK), BF16),
             pltpu.VMEM((2 * length, CHUNK), BF16),
             pltpu.VMEM((2 * length, CHUNK), BF16),
             pltpu.VMEM((8, LANES), BF16),
+            pltpu.VMEM((groups, state, CHUNK), F32),
+            pltpu.VMEM((groups, state + 8, CHUNK), F32),
+            pltpu.VMEM((groups, state + 8, CHUNK), F32),
+            pltpu.VMEM((groups - 1, state + 8, CHUNK), F32),
+            pltpu.VMEM((groups, state + 8, CHUNK), F32),
+            pltpu.VMEM((groups, state, CHUNK), F32),
+            pltpu.VMEM((groups, state, CHUNK), F32),
+            pltpu.VMEM((groups, state, CHUNK), F32),
+            dma((2, groups)),
+            dma((groups,)), dma((groups,)),
+            dma((groups,)), dma((groups,)),
+            dma((groups,)), dma((groups,)),
+            dma((groups,)), dma((groups,)),
         ],
-        compiler_params=pltpu.CompilerParams(vmem_limit_bytes=VMEM_LIMIT, dimension_semantics=("arbitrary",)),
+        compiler_params=pltpu.CompilerParams(vmem_limit_bytes=VMEM_LIMIT, collective_id=0, has_side_effects=True),
         cost_estimate=pl.CostEstimate(flops=8 * length * width * state, bytes_accessed=4 * length * width, transcendentals=0),
     )(x, y, bc, dt, bias, alog)
 
 
-def main_kernel(heads, xf_ref, yf_ref, xb_ref, yb_ref, bc_ref, dt_ref, bias_ref, alog_ref, skip_ref, hin_ref, gin_ref,
+def main_kernel(heads, zs, dps, flats, scale, xf_ref, yf_ref, xb_ref, yb_ref, bc_ref, dt_ref, bias_ref, alog_ref, skip_ref, hin_ref, gin_ref,
                 gx_ref, gbc_ref, gdt_ref, gheads_ref,
-                pe, pf, dts, shs, sel, rows, vs, ws, zf, zb, ll, xx, prods, hst, gst, yx):
-    length = dt_ref.shape[0]
+                pe, pf, dts, shs, sel, rows, vs, ws, zf, zb, ll, xx, prods, hst, gst, yx,
+                part, stage, landed, done, hsum, hgot, s1, r1s, s2, r2s, s3, r3s):
+    length = dts.shape[0]
     width = sel.shape[1]
     blocks = length // Q
     step = pl.program_id(0)
     kf = step
     kb = blocks - 1 - step
     chunks = [slice(c * CHUNK, (c + 1) * CHUNK) for c in range(width // CHUNK)]
-    rate = -jnp.exp(repeat_heads(jnp.broadcast_to(alog_ref[...], (8, heads)), heads))[:1]
+    rate = rates_of(alog_ref, heads)
+    half = blocks // 2
+    lines = Q // zs
+    z = lax.axis_index("head")
+    flat = lax.axis_index("seq") * dps + lax.axis_index("dp")
+    barrier = pltpu.get_barrier_semaphore()
+
+    def zpeer(d):
+        return {"head": lax.rem(z + d, zs)}
+
+    def fpeer(d):
+        other = lax.rem(flat + d, flats)
+        return {"seq": other // dps, "dp": lax.rem(other, dps)}
+
+    def scatter(j, d):
+        q = lax.rem(z + d, zs)
+        return pltpu.make_async_remote_copy(
+            src_ref=stage.at[j, q], dst_ref=landed.at[j, z], send_sem=s1.at[j, q], recv_sem=r1s.at[j, z],
+            device_id=zpeer(d), device_id_type=pl.DeviceIdType.MESH)
+
+    def scatter_in(j, d):
+        q = lax.rem(z + d, zs)
+        return pltpu.make_async_remote_copy(
+            src_ref=stage.at[j, q], dst_ref=landed.at[j, q], send_sem=s1.at[j, q], recv_sem=r1s.at[j, q],
+            device_id=zpeer(d), device_id_type=pl.DeviceIdType.MESH)
+
+    def gather(j, d):
+        q = lax.rem(z + d, zs)
+        return pltpu.make_async_remote_copy(
+            src_ref=done.at[j, z], dst_ref=done.at[j, z], send_sem=s2.at[j, q], recv_sem=r2s.at[j, z],
+            device_id=zpeer(d), device_id_type=pl.DeviceIdType.MESH)
+
+    def gather_in(j, d):
+        q = lax.rem(z + d, zs)
+        return pltpu.make_async_remote_copy(
+            src_ref=done.at[j, q], dst_ref=done.at[j, q], send_sem=s2.at[j, q], recv_sem=r2s.at[j, q],
+            device_id=zpeer(d), device_id_type=pl.DeviceIdType.MESH)
+
+    def share(d):
+        return pltpu.make_async_remote_copy(
+            src_ref=hsum, dst_ref=hgot.at[flat], send_sem=s3.at[d], recv_sem=r3s.at[flat],
+            device_id=fpeer(d), device_id_type=pl.DeviceIdType.MESH)
+
+    def share_in(d):
+        other = lax.rem(flat + d, flats)
+        return pltpu.make_async_remote_copy(
+            src_ref=hsum, dst_ref=hgot.at[other], send_sem=s3.at[d], recv_sem=r3s.at[other],
+            device_id=fpeer(d), device_id_type=pl.DeviceIdType.MESH)
+
+    def reduce_pair(j):
+        for d in range(1, zs):
+            scatter_in(j, d).wait_recv()
+        landed[j, z] = stage[j, z]
+        total = landed[j, 0]
+        for q in range(1, zs):
+            total = total + landed[j, q]
+        done[j, z] = total
+        for d in range(1, zs):
+            gather(j, d).start()
+
+    def finish_pair(j):
+        for d in range(1, zs):
+            gather_in(j, d).wait_recv()
+        for q in range(zs):
+            gbc_ref[pl.ds(pl.multiple_of((half + j) * Q + q * lines, lines), lines), :] = done[j, q, :lines]
+            gbc_ref[pl.ds(pl.multiple_of((half - 1 - j) * Q + q * lines, lines), lines), :] = done[j, q, lines:]
 
     @pl.when(step == 0)
     def _():
+        for d in range(1, zs):
+            pl.semaphore_signal(barrier, inc=1, device_id=zpeer(d), device_id_type=pl.DeviceIdType.MESH)
+
+        @pl.loop(1, flats)
+        def _(d):
+            pl.semaphore_signal(barrier, inc=1, device_id=fpeer(d), device_id_type=pl.DeviceIdType.MESH)
+
         sel[...] = head_lanes(heads, width)
-        shifted = repeat_heads(dt_ref[...] + bias_ref[...], heads)
+        shifted = steps_of(dt_ref, bias_ref, heads)
         shs[...] = shifted
         dt = jax.nn.softplus(shifted)
         dts[...] = dt
@@ -171,12 +382,12 @@
         skips = repeat_heads(jnp.broadcast_to(skip_ref[...], (8, heads)), heads)
         rows[blocks] = dot_nn(packed(skips, heads, 3), sel[...])
         yx[...] = jnp.zeros_like(yx)
-        gbc_ref[...] = jnp.zeros_like(gbc_ref)
-        for c in chunks:
-            h = hin_ref[:, c] * rows[0, 1:2, c]
+        part[...] = jnp.zeros_like(part)
+        for i, c in enumerate(chunks):
+            h = hin_ref[i] * rows[0, 1:2, c]
             hst[:, c] = h
             zf[0:128, c], zf[256:384, c] = halves(h)
-            g = gin_ref[:, c] * rows[blocks - 1, 0:1, c]
+            g = gin_ref[i] * rows[blocks - 1, 0:1, c]
             gst[:, c] = g
             zb[0:128, c], zb[256:384, c] = halves(g)
 
@@ -235,11 +446,11 @@
     grad_c = r1[:64, :128] + r1[64:, :128] + r2 + dot_nn(p_hi, b_ff) + dot_nn(p_lo, b_ff)
     turned = jnp.transpose(pair)
     t_hi, t_lo = halves(turned[:64] + turned[64:])
-    gbc_ref[spanf, LANES:] = grad_c
-    gbc_ref[spanf, :LANES] += dot_nn(t_hi, c_f) + dot_nn(t_lo, c_f)
+    part[spanf, LANES:] = grad_c
+    part[spanf, :LANES] += dot_nn(t_hi, c_f) + dot_nn(t_lo, c_f)
     r1 = dot_nt(xx[...], zb[0:128, :])
     r2 = dot_nt(xx[0:64, :], zb[256:384, :])
-    gbc_ref[spanb, :LANES] += r1[:64] + r1[64:] + r2
+    part[spanb, :LANES] += r1[:64] + r1[64:] + r2
 
     bt = jnp.transpose(b_ff.astype(F32)).astype(BF16)
     ct = jnp.transpose(c_bb.astype(F32)).astype(BF16)
@@ -253,13 +464,36 @@
         gst[:, c] = g
         zb[0:128, c], zb[256:384, c] = halves(g)
 
+    @pl.when(step == half)
+    def _():
+        pl.semaphore_wait(barrier, zs - 1 + flats - 1)
+
+    @pl.when(step >= half)
+    def _():
+        j = step - half
+        for q in range(zs):
+            stage[j, q, :lines] = part[pl.ds(pl.multiple_of(kf * Q + q * lines, lines), lines), :]
+            stage[j, q, lines:] = part[pl.ds(pl.multiple_of(kb * Q + q * lines, lines), lines), :]
+        for d in range(1, zs):
+            scatter(j, d).start()
+
+    @pl.when(step >= half + 1)
+    def _():
+        reduce_pair(step - half - 1)
+
+    @pl.when(step >= half + 2)
+    def _():
+        finish_pair(step - half - 2)
+
     @pl.when(step == blocks - 1)
     def _():
-        closing = jnp.sum(gin_ref[...] * hst[...], axis=0, keepdims=True)
+        closing = jnp.concatenate(
+            [jnp.sum(gin_ref[i] * hst[:, c], axis=0, keepdims=True) for i, c in enumerate(chunks)], axis=1)
         totals = jnp.concatenate([closing, jnp.sum(yx[...], axis=0, keepdims=True), jnp.zeros((14, width), F32)], axis=0)
         hi, lo = halves(totals)
         totals = dot_nt(hi, sel[...]) + dot_nt(lo, sel[...])
         after = totals[0:1]
+        gdts = []
         tri = triangle(True)
         d_alog = jnp.zeros((1, LANES), F32)
         d_bias = jnp.zeros((1, LANES), F32)
@@ -270,28 +504,61 @@
             dlog = dot_nn(tri, vs[span] - w, HIGH) + after
             after = dlog[0:1]
             grad_dt = (w / dt + dlog * rate) * jax.nn.sigmoid(shs[span])
-            gdt_ref[span, :] = grad_dt[:, :heads]
+            gdts.append(grad_dt)
             d_alog = d_alog + jnp.sum(dlog * dt, axis=0, keepdims=True)
             d_bias = d_bias + jnp.sum(grad_dt, axis=0, keepdims=True)
-        gheads_ref[...] = jnp.concatenate(
-            [d_alog * rate, d_bias, totals[1:2], jnp.zeros((5, LANES), F32)], axis=0)
+        hsum[...] = jnp.concatenate([d_alog * rate, d_bias, totals[1:2], jnp.zeros((5, LANES), F32)], axis=0)
+
+        @pl.loop(1, flats)
+        def _(d):
+            share(d).start()
+
+        reduce_pair(half - 1)
+        gdt_ref[...] = jnp.transpose(jnp.concatenate(gdts[::-1], axis=0))[:heads]
+        finish_pair(half - 2)
+        hgot[flat] = hsum[...]
+
+        @pl.loop(1, flats)
+        def _(d):
+            share_in(d).wait_recv()
+
+        total = hgot[0]
+        for other in range(1, flats):
+            total = total + hgot[other]
+        gheads_ref[...] = total * scale
+        finish_pair(half - 1)
+
+        @pl.loop(1, flats)
+        def _(d):
+            share(d).wait_send()
+
+        @pl.loop(0, half)
+        def _(j):
+            for d in range(1, zs):
+                scatter(j, d).wait_send()
+                gather(j, d).wait_send()
 
 
 def main(x, y, bc, dt, bias, alog, skip, hin, gin):
     length, width = x.shape
-    heads = dt.shape[1]
+    heads = dt.shape[0]
     state = bc.shape[1] // 2
     blocks = length // Q
+    zs, dps = lax.axis_size("head"), lax.axis_size("dp")
+    flats = lax.axis_size("seq") * dps
+    scale = 1.0 / math.sqrt(flats * length)
+    lines = Q // zs
+    dma = pltpu.SemaphoreType.DMA
     whole = pl.BlockSpec(memory_space=pltpu.VMEM)
     ahead = pl.BlockSpec((Q, width), lambda i: (i, 0))
     back = pl.BlockSpec((Q, width), lambda i: (blocks - 1 - i, 0))
     return pl.pallas_call(
-        functools.partial(main_kernel, heads),
+        functools.partial(main_kernel, heads, zs, dps, flats, scale),
         grid=(blocks,),
         out_shape=(
             jax.ShapeDtypeStruct((length, width), BF16),
             jax.ShapeDtypeStruct((length, 2 * state), F32),
-            jax.ShapeDtypeStruct((length, heads), F32),
+            jax.ShapeDtypeStruct((heads, length), F32),
             jax.ShapeDtypeStruct((8, LANES), F32),
         ),
         in_specs=[ahead, ahead, back, back] + [whole] * 7,
@@ -313,39 +580,29 @@
             pltpu.VMEM((state, width), F32),
             pltpu.VMEM((state, width), F32),
             pltpu.VMEM((8, width), F32),
+            pltpu.VMEM((length, 2 * state), F32),
+            pltpu.VMEM((blocks // 2, zs, 2 * lines, 2 * state), F32),
+            pltpu.VMEM((blocks // 2, zs, 2 * lines, 2 * state), F32),
+            pltpu.VMEM((blocks // 2, zs, 2 * lines, 2 * state), F32),
+            pltpu.VMEM((8, LANES), F32),
+            pltpu.VMEM((flats, 8, LANES), F32),
+            dma((blocks // 2, zs)), dma((blocks // 2, zs)),
+            dma((blocks // 2, zs)), dma((blocks // 2, zs)),
+            dma((flats,)), dma((flats,)),
         ],
-        compiler_params=pltpu.CompilerParams(vmem_limit_bytes=VMEM_LIMIT, dimension_semantics=("arbitrary",)),
+        compiler_params=pltpu.CompilerParams(
+            vmem_limit_bytes=VMEM_LIMIT, collective_id=1, has_side_effects=True, dimension_semantics=("arbitrary",)),
         cost_estimate=pl.CostEstimate(flops=60 * length * width * state, bytes_accessed=12 * length * width, transcendentals=0),
     )(x, y, x, y, bc, dt, bias, alog, skip, hin, gin)
 
 
-def carried_in(decay, value, axis, reverse):
-    count, place = (lax.axis_size(axis), lax.axis_index(axis))
-    decays = lax.all_gather(decay, axis)
-    values = lax.all_gather(value, axis)
-
-    def hop(k, before):
-        at = count - 1 - k if reverse else k
-        reached = at > place if reverse else at < place
-        return jnp.where(reached, decays[at] * before + values[at], before)
-
-    return lax.fori_loop(0, count, hop, jnp.zeros_like(value))
-
-
 def shards(inputs_x, inputs_bc, dt_raw, grad_out, a_log, dt_bias, skip):
-    length = inputs_x.shape[1]
     heads = a_log.shape[0]
-    x, y, bc, dt = inputs_x[0], grad_out[0], inputs_bc[0], dt_raw[0]
+    x, y, bc, dt = inputs_x[0], grad_out[0], inputs_bc[0], dt_raw[0].T
     bias, alog, skips = dt_bias[None], a_log[None], skip[None]
-    ends, starts, decay = edges(x, y, bc, dt, bias, alog)
-    hin = carried_in(decay[:1], ends, "seq", False)
-    gin = carried_in(decay[:1], starts, "seq", True)
+    hin, gin = edges(x, y, bc, dt, bias, alog)
     grad_x, grad_bc, grad_dt, sums = main(x, y, bc, dt, bias, alog, skips, hin, gin)
-    grad_bc = lax.psum(grad_bc, "head")
-    sequences = inputs_x.shape[0] * lax.axis_size("dp")
-    scale = 1.0 / math.sqrt(sequences * length * lax.axis_size("seq"))
-    grad_heads = lax.psum(sums[:3, :heads], ("seq", "dp")) * scale
-    return (grad_x[None], grad_bc[None], grad_dt[None], grad_heads)
+    return (grad_x[None], grad_bc[None], grad_dt.T[None], sums[:3, :heads])
 
 
 def solution(mesh):

time: 429 us -> 143 us (0.33)
  waiting for transfers between devices: 161 us -> 0 us
  blocking collectives: 89.4 us -> 0 us
  other arithmetic: 69.2 us -> 0 us
  Pallas kernels: 85.7 us -> 134 us
  between operations: 13.8 us -> 0.65 us
    all_gather x2 -> x0, waiting for transfers between devices: 160 us -> none  [carried_in(): values = lax.all_gather(value, axis)]
    select_n x32 -> x0, other arithmetic: 68.6 us -> none  [hop(): return jnp.where(reached, decays[at] * before + values[at], before)]
    psum x1 -> x0, blocking collectives: 63.9 us -> none  [shards(): grad_heads = lax.psum(sums[:3, :heads], ('seq', 'dp')) * scale]
    pallas_call x2, Pallas kernels: 85.7 us -> 134 us  [the longest x1 88.5 us: main(): pl.pallas_call(functools.partial(main_kernel, heads, zs, dps, flats, scal...]
    all_gather x1 -> x0, blocking collectives: 25.4 us -> none  [carried_in(): decays = lax.all_gather(decay, axis)]
  transfers between devices with their start and end apart: 3 -> 0, of which waited for: 2 -> 0; matrix products, arithmetic and copies ran while one was open for 9% -> 0% of each run, Pallas kernels for 0% -> 0%
where the time goes in v2:
time: 143 us; the launch traced here: 142 us
  Pallas kernels  134 us (94%)
  local copies, waits for them, and re-layouts  7.77 us (5%)
    pallas_call x1, Pallas kernels, main(): pl.pallas_call(functools.partial(main_kernel, heads, zs, dps, flats, scal...  88.5 us
    pallas_call x1, Pallas kernels, edges(): pl.pallas_call(functools.partial(edges_kernel, heads), out_shape=(jax.Sha...  45.5 us
    unnamed x7, local copies, waits for them, and re-layouts  6.52 us

profile of v2, /device:TPU:0, one launch (start us, length us, event | category | flops | bytes accessed | tf_op | source)
XLA Modules:
  0.0 142.4 jit_solution(10628099819107548478)
XLA Ops:
  0.6 45.5 %shard_map.102 = (f32[8,128,256]{2,1,0:T(8,128)}, f32[8,128,256]{2,1,0:T(8,128)}) custom-call(bf16[1024,2048]{1,0:T(8,128)(2,1)} %bitcast.14, bf16[1024,2048]{1,0:T(8,128)(2,1)} %bitcast.17, bf16[1024,256]{1,0:T(8,128)(2,1)} %bitcast.22, f32[32,1024]{1,0:T(8,128)} %bitcast.24, f32[1,32]{1,0:T(1,128)} %bitcast.27, f32[1,32]{1,0:T(1,128)} %bitcast.29), custom_call_target="tpu_custom_call" | custom-call | flops 2147483648 | bytes 8388608 | tf_op jit(solution)/shard_map/pallas_call | solution.py:237
  46.1 88.5 %shard_map.103 = (bf16[1024,2048]{1,0:T(8,128)(2,1)}, f32[1024,256]{1,0:T(8,128)}, f32[32,1024]{1,0:T(8,128)}, f32[8,128]{1,0:T(8,128)}) custom-call(bf16[1024,2048]{1,0:T(8,128)(2,1)} %bitcast.15, bf16[1024,2048]{1,0:T(8,128)(2,1)} %bitcast.18, bf16[1024,2048]{1,0:T(8,128)(2,1)} %bitcast.16, bf16[1024,2048]{1,0:T(8,128)(2,1)} %bitcast.19, ...), custom_call_target="tpu_custom_call" | custom-call | flops 16106127360 | bytes 25165824 | tf_op jit(solution)/shard_map/pallas_call | solution.py:555
  134.6 1.3 slice.3
  135.8 0.0 copy-start
  135.8 0.0 copy-start.1
  135.9 4.9 %copy.14 = bf16[1,1024,2048]{2,1,0:T(8,128)(2,1)} copy(bf16[1,1024,2048]{2,1,0:T(8,128)(2,1)} %bitcast.20) | data formatting | bytes 8388608
  140.7 0.0 copy-done
  140.7 1.0 copy.15
  141.7 0.0 copy-done.1
  141.7 0.7 copy.16
Async XLA Ops:
  135.8 4.9 %copy-start = (f32[1024,256]{1,0:T(8,128)S(1)}, f32[1024,256]{1,0:T(8,128)}, u32[]{:S(2)}) copy-start(f32[1024,256]{1,0:T(8,128)} %get-tuple-element.13) | copy-start | bytes 3145732
  135.8 5.9 %copy-start.1 = (f32[32,1024]{1,0:T(8,128)S(1)}, f32[32,1024]{1,0:T(8,128)}, u32[]{:S(2)}) copy-start(f32[32,1024]{1,0:T(8,128)} %get-tuple-element.14) | copy-start | bytes 393220

commit v3 on v2

--- a/solution.py
+++ b/solution.py
@@ -70,9 +70,11 @@
     return -jnp.exp(repeat_heads(jnp.broadcast_to(alog_ref[...], (8, heads)), heads))[:1]
 
 
-def edges_kernel(heads, x_ref, y_ref, bc_ref, dt_ref, bias_ref, alog_ref, hin_ref, gin_ref,
-                 pe, pf, bt, ct, sel, xb, yb, xs, ys, dec, mine, out0, got0, chip, gath, pre, inc, fin,
-                 load_sem, s0, r0, s1, r1, s2, r2, s3, r3):
+def edges_kernel(heads, x_ref, y_ref, bc_ref, dt_ref, bias_ref, alog_ref,
+                 hin_ref, gin_ref, skip_ref, xo_ref, lo_ref, fo_ref, af_ref, ab_ref, part_ref,
+                 pe, pf, le, lf, bt, ct, sel, xb, yb, xs, ys, dec, mine, out0, got0, chip, gath, pre, inc, fin,
+                 xbuf, lbuf, fbuf, abuf, bbuf, part, yx,
+                 load_sem, s0, r0, s1, r1, s2, r2, s3, r3, put_sem, put_one):
     length = bc_ref.shape[0]
     blocks = length // Q
     groups = hin_ref.shape[0]
@@ -137,6 +139,9 @@
     cums = [dot_nn(tri, dt[k * Q:(k + 1) * Q] * rate, HIGH) for k in range(blocks)]
     before = jnp.zeros((1, LANES), F32)
     for k in range(blocks):
+        mid = cums[k][Q // 2 - 1:Q // 2]
+        le[pl.ds(k * Q, Q), :] = packed(jnp.exp(cums[k] - mid), heads, 2)
+        lf[pl.ds(k * Q, Q), :] = packed(dt[k * Q:(k + 1) * Q] * jnp.exp(mid - cums[k]), heads, 2)
         pe[pl.ds(k * Q, Q), :] = packed(jnp.exp(cums[k] + before), heads, 2)
         before = before + cums[k][Q - 1:Q]
     after = jnp.zeros((1, LANES), F32)
@@ -188,22 +193,86 @@
             combine(i - 1)
     combine(groups - 1)
 
-    total = jnp.zeros((state, CHUNK), F32)
-    for d in range(1, groups):
-        spread_in(peer(d)).wait_recv()
-    for k in range(groups):
-        pos = jnp.where(ahead, k, groups - 1 - k)
-
-        @pl.when(pos == place)
-        def _():
-            inc[place] = total
-
-        @pl.when(pos != place)
-        def _():
-            pre[pos] = total
-            back(pos).start()
-
-        total = gath[pos, state:state + 1, :] * total + gath[pos, :state, :]
+    def scan():
+        total = jnp.zeros((state, CHUNK), F32)
+        for d in range(1, groups):
+            spread_in(peer(d)).wait_recv()
+        for k in range(groups):
+            pos = jnp.where(ahead, k, groups - 1 - k)
+
+            @pl.when(pos == place)
+            def _():
+                inc[place] = total
+
+            @pl.when(pos != place)
+            def _():
+                pre[pos] = total
+                back(pos).start()
+
+            total = gath[pos, state:state + 1, :] * total + gath[pos, :state, :]
+
+    def puts(i):
+        g = peer(1 + i)
+        span = pl.ds(pl.multiple_of(g * CHUNK, CHUNK), CHUNK)
+        return (pltpu.make_async_copy(xbuf.at[:, :, span], xo_ref.at[:, :, span], put_sem.at[0, i]),
+                pltpu.make_async_copy(lbuf.at[:, :, span], lo_ref.at[:, :, span], put_sem.at[1, i]),
+                pltpu.make_async_copy(fbuf.at[:, span], fo_ref.at[:, span], put_sem.at[2, i]))
+
+    for i in range(groups):
+        g = peer(1 + i)
+        span = pl.ds(pl.multiple_of(g * CHUNK, CHUNK), CHUNK)
+        here = sel[:, span]
+        x = xb[i].astype(F32)
+        y = yb[i].astype(F32)
+        f = dot_nn(lf[...], here)
+        fbuf[:, span] = f
+        hi, lo = halves(f * x)
+        xbuf[:, :Q, span] = lo.reshape(blocks, Q, CHUNK)
+        xbuf[:, Q:, span] = hi.reshape(blocks, Q, CHUNK)
+        hi, lo = halves(dot_nn(le[...], here) * y)
+        lbuf[:, :Q, span] = lo.reshape(blocks, Q, CHUNK)
+        lbuf[:, Q:, span] = hi.reshape(blocks, Q, CHUNK)
+        yx[:, span] = jnp.sum((y * x).reshape(length // 8, 8, CHUNK), axis=0)
+        for copy in puts(i):
+            copy.start()
+        if i == groups // 2:
+            scan()
+
+    lane = iota((Q, 2 * Q), 1)
+    row = iota((Q, 2 * Q), 0)
+    none = jnp.zeros((Q, 2 * Q), F32)
+
+    @pl.loop(0, blocks)
+    def _(k):
+        span = pl.ds(pl.multiple_of(k * Q, Q), Q)
+        b, c = bc_ref[span, :LANES], bc_ref[span, LANES:]
+        bb = jnp.concatenate([b, b], axis=0)
+        cc = jnp.concatenate([c, c], axis=0)
+        lower = row >= lane % Q
+        for dest, one, two, keep in ((abuf, c, bb, lower), (bbuf, b, cc, row <= lane % Q)):
+            s_hi, s_lo = halves(jnp.where(keep, dot_nt(one, two), none))
+            dest[k, :Q, :2 * Q] = one
+            dest[k, :Q, 2 * Q:] = s_hi
+            dest[k, Q:3 * Q, :2 * Q] = jnp.zeros((2 * Q, 2 * Q), BF16)
+            dest[k, Q:3 * Q, 2 * Q:] = jnp.transpose(two.astype(F32)).astype(BF16)
+            dest[k, 3 * Q:, :2 * Q] = s_lo
+            dest[k, 3 * Q:, 2 * Q:] = one
+        r = dot_nt(lbuf[k], xbuf[k])
+        pair = jnp.where(lower, r[:Q] + r[Q:], none)
+        p_hi, p_lo = halves(pair)
+        part[span, LANES:] = dot_nn(p_hi, bb) + dot_nn(p_lo, bb)
+        turned = jnp.transpose(pair)
+        t_hi, t_lo = halves(turned[:Q] + turned[Q:])
+        part[span, :LANES] = dot_nn(t_hi, c) + dot_nn(t_lo, c)
+
+    put_all = (pltpu.make_async_copy(abuf, af_ref, put_one.at[0]),
+               pltpu.make_async_copy(bbuf, ab_ref, put_one.at[1]),
+               pltpu.make_async_copy(part, part_ref, put_one.at[2]))
+    for copy in put_all:
+        copy.start()
+    sums = jnp.sum(yx[...], axis=0, keepdims=True)
+    hi, lo = halves(jnp.broadcast_to(sums, yx.shape))
+    skip_ref[...] = dot_nt(hi, sel[...]) + dot_nt(lo, sel[...])
 
     for d in range(groups):
         g = peer(d)
@@ -224,6 +293,11 @@
     for d in range(1, groups):
         spread(d).wait_send()
         back(peer(d)).wait_send()
+    for i in range(groups):
+        for copy in puts(i):
+            copy.wait()
+    for copy in put_all:
+        copy.wait()
 
 
 def edges(x, y, bc, dt, bias, alog):
@@ -231,6 +305,7 @@
     heads = dt.shape[0]
     state = bc.shape[1] // 2
     groups = width // CHUNK
+    blocks = length // Q
     whole = pl.BlockSpec(memory_space=pltpu.VMEM)
     anywhere = pl.BlockSpec(memory_space=pl.ANY)
     dma = pltpu.SemaphoreType.DMA
@@ -239,10 +314,19 @@
         out_shape=(
             jax.ShapeDtypeStruct((groups, state, CHUNK), F32),
             jax.ShapeDtypeStruct((groups, state, CHUNK), F32),
+            jax.ShapeDtypeStruct((8, LANES), F32),
+            jax.ShapeDtypeStruct((blocks, 2 * Q, width), BF16),
+            jax.ShapeDtypeStruct((blocks, 2 * Q, width), BF16),
+            jax.ShapeDtypeStruct((length, width), F32),
+            jax.ShapeDtypeStruct((blocks, 4 * Q, 4 * Q), BF16),
+            jax.ShapeDtypeStruct((blocks, 4 * Q, 4 * Q), BF16),
+            jax.ShapeDtypeStruct((length, 2 * state), F32),
         ),
         in_specs=[anywhere, anywhere, whole, whole, whole, whole],
-        out_specs=(whole, whole),
+        out_specs=(whole, whole, whole) + (anywhere,) * 6,
         scratch_shapes=[
+            pltpu.VMEM((length, LANES), BF16),
+            pltpu.VMEM((length, LANES), BF16),
             pltpu.VMEM((length, LANES), BF16),
             pltpu.VMEM((length, LANES), BF16),
             pltpu.VMEM((state, 2 * length), BF16),
@@ -261,21 +345,30 @@
             pltpu.VMEM((groups, state, CHUNK), F32),
             pltpu.VMEM((groups, state, CHUNK), F32),
             pltpu.VMEM((groups, state, CHUNK), F32),
+            pltpu.VMEM((blocks, 2 * Q, width), BF16),
+            pltpu.VMEM((blocks, 2 * Q, width), BF16),
+            pltpu.VMEM((length, width), F32),
+            pltpu.VMEM((blocks, 4 * Q, 4 * Q), BF16),
+            pltpu.VMEM((blocks, 4 * Q, 4 * Q), BF16),
+            pltpu.VMEM((length, 2 * state), F32),
+            pltpu.VMEM((8, width), F32),
             dma((2, groups)),
             dma((groups,)), dma((groups,)),
             dma((groups,)), dma((groups,)),
             dma((groups,)), dma((groups,)),
             dma((groups,)), dma((groups,)),
+            dma((3, groups)), dma((3,)),
         ],
         compiler_params=pltpu.CompilerParams(vmem_limit_bytes=VMEM_LIMIT, collective_id=0, has_side_effects=True),
         cost_estimate=pl.CostEstimate(flops=8 * length * width * state, bytes_accessed=4 * length * width, transcendentals=0),
     )(x, y, bc, dt, bias, alog)
 
 
-def main_kernel(heads, zs, dps, flats, scale, xf_ref, yf_ref, xb_ref, yb_ref, bc_ref, dt_ref, bias_ref, alog_ref, skip_ref, hin_ref, gin_ref,
+def main_kernel(heads, zs, dps, flats, scale, xf_ref, lf_ref, xb_ref, lb_ref, fb_ref, yb_ref, af_ref, ab_ref,
+                part_ref, dskip_ref, dt_ref, bias_ref, alog_ref, skip_ref, hin_ref, gin_ref,
                 gx_ref, gbc_ref, gdt_ref, gheads_ref,
-                pe, pf, dts, shs, sel, rows, vs, ws, zf, zb, ll, xx, prods, hst, gst, yx,
-                part, stage, landed, done, hsum, hgot, s1, r1s, s2, r2s, s3, r3s):
+                dts, shs, sel, rows, vs, ws, hz, gz, prods, hst, gst,
+                stage, landed, done, hsum, hgot, s1, r1s, s2, r2s, s3, r3s):
     length = dts.shape[0]
     width = sel.shape[1]
     blocks = length // Q
@@ -284,7 +377,6 @@
     kb = blocks - 1 - step
     chunks = [slice(c * CHUNK, (c + 1) * CHUNK) for c in range(width // CHUNK)]
     rate = rates_of(alog_ref, heads)
-    half = blocks // 2
     lines = Q // zs
     z = lax.axis_index("head")
     flat = lax.axis_index("seq") * dps + lax.axis_index("dp")
@@ -347,8 +439,8 @@
         for d in range(1, zs):
             gather_in(j, d).wait_recv()
         for q in range(zs):
-            gbc_ref[pl.ds(pl.multiple_of((half + j) * Q + q * lines, lines), lines), :] = done[j, q, :lines]
-            gbc_ref[pl.ds(pl.multiple_of((half - 1 - j) * Q + q * lines, lines), lines), :] = done[j, q, lines:]
+            gbc_ref[pl.ds(pl.multiple_of(j * Q + q * lines, lines), lines), LANES:] = done[j, q, :lines]
+            gbc_ref[pl.ds(pl.multiple_of((blocks - 1 - j) * Q + q * lines, lines), lines), :LANES] = done[j, q, lines:]
 
     @pl.when(step == 0)
     def _():
@@ -370,8 +462,6 @@
             here = dt[k * Q:(k + 1) * Q]
             cum = dot_nn(tri, here * rate, HIGH)
             mid = cum[Q // 2 - 1:Q // 2]
-            pe[pl.ds(k * Q, Q), :] = packed(jnp.exp(cum - mid), heads, 2)
-            pf[pl.ds(k * Q, Q), :] = packed(here * jnp.exp(mid - cum), heads, 2)
             mids.append(mid)
             lasts.append(cum[Q - 1:Q])
         for k in range(blocks):
@@ -381,116 +471,75 @@
             rows[k] = dot_nn(factor, sel[...])
         skips = repeat_heads(jnp.broadcast_to(skip_ref[...], (8, heads)), heads)
         rows[blocks] = dot_nn(packed(skips, heads, 3), sel[...])
-        yx[...] = jnp.zeros_like(yx)
-        part[...] = jnp.zeros_like(part)
         for i, c in enumerate(chunks):
             h = hin_ref[i] * rows[0, 1:2, c]
             hst[:, c] = h
-            zf[0:128, c], zf[256:384, c] = halves(h)
+            hz[0, :128, c], hz[0, 128:, c] = halves(h)
             g = gin_ref[i] * rows[blocks - 1, 0:1, c]
             gst[:, c] = g
-            zb[0:128, c], zb[256:384, c] = halves(g)
+            gz[0, :128, c], gz[0, 128:, c] = halves(g)
 
     spanf = pl.ds(pl.multiple_of(kf * Q, Q), Q)
     spanb = pl.ds(pl.multiple_of(kb * Q, Q), Q)
-    lane = iota((Q, 2 * Q), 1)
-    row = iota((Q, 2 * Q), 0)
-
-    b_f, c_f = bc_ref[spanf, :LANES], bc_ref[spanf, LANES:]
-    b_b, c_b = bc_ref[spanb, :LANES], bc_ref[spanb, LANES:]
-    b_ff = jnp.concatenate([b_f, b_f], axis=0)
-    c_bb = jnp.concatenate([c_b, c_b], axis=0)
-    zero = jnp.zeros((Q, 2 * Q), F32)
-
-    lower = row >= lane % Q
-    s_hi, s_lo = halves(jnp.where(lower, dot_nt(c_f, b_ff), zero))
-    first_f = jnp.concatenate([c_f, s_hi], axis=1)
-    second_f = jnp.concatenate([s_lo, c_f], axis=1)
-    upper = row <= lane % Q
-    s_hi, s_lo = halves(jnp.where(upper, dot_nt(b_b, c_bb), zero))
-    first_b = jnp.concatenate([b_b, s_hi], axis=1)
-    second_b = jnp.concatenate([s_lo, b_b], axis=1)
-
+    now = lax.rem(step, 2)
+    first_f, second_f = af_ref[0, :192], af_ref[0, 192:]
+    first_b, second_b = ab_ref[0, :192], ab_ref[0, 192:]
+    come_f = jnp.minimum(kf + 1, blocks - 1)
+    come_b = jnp.maximum(kb - 1, 0)
+    last = step == blocks - 1
     for c in chunks:
-        e = dot_nn(pe[spanf, :], sel[:, c])
-        f = dot_nn(pf[spanf, :], sel[:, c])
-        lifted = e * yf_ref[:, c].astype(F32)
-        xs = f * xf_ref[:, c].astype(F32)
-        zf[192:256, c], zf[128:192, c] = halves(xs)
-        ll[0:64, c], ll[64:128, c] = halves(lifted)
-        out = dot_nn(first_f, zf[0:256, c]) + dot_nn(second_f, zf[128:384, c])
-        prods[0:64, c], prods[64:128, c] = halves(lifted * out)
-
-        e = dot_nn(pe[spanb, :], sel[:, c])
-        f = dot_nn(pf[spanb, :], sel[:, c])
-        y = yb_ref[:, c].astype(F32)
-        x = xb_ref[:, c].astype(F32)
-        lifted = e * y
-        xs = f * x
-        zb[192:256, c], zb[128:192, c] = halves(lifted)
-        xx[0:64, c], xx[64:128, c] = halves(xs)
-        out = dot_nn(first_b, zb[0:256, c]) + dot_nn(second_b, zb[128:384, c])
+        wide = xf_ref[0, :, c]
+        one = dot_nn(first_f, jnp.concatenate([hz[now, :128, c], wide], axis=0))
+        two = dot_nn(second_f, jnp.concatenate([wide, hz[now, 128:, c]], axis=0))
+        lifted = lf_ref[0, 64:, c].astype(F32) + lf_ref[0, :64, c].astype(F32)
+        prods[0:64, c], prods[64:128, c] = halves(lifted * (one[:64] + two))
+        h = (hst[:, c] + one[64:]) * rows[kf, 0:1, c] * jnp.where(last, 1.0, rows[come_f, 1:2, c])
+        hst[:, c] = h
+        hz[1 - now, :128, c], hz[1 - now, 128:, c] = halves(h)
+
+        wide = lb_ref[0, :, c]
+        one = dot_nn(first_b, jnp.concatenate([gz[now, :128, c], wide], axis=0))
+        two = dot_nn(second_b, jnp.concatenate([wide, gz[now, 128:, c]], axis=0))
+        out = one[:64] + two
+        xs = xb_ref[0, 64:, c].astype(F32) + xb_ref[0, :64, c].astype(F32)
         prods[128:192, c], prods[192:256, c] = halves(xs * out)
-        gx_ref[:, c] = (f * out + rows[blocks, :1, c] * y).astype(BF16)
-        yx[:, c] += jnp.sum((y * x).reshape(Q // 8, 8, CHUNK), axis=0)
+        gx_ref[:, c] = (fb_ref[:, c] * out + rows[blocks, :1, c] * yb_ref[:, c].astype(F32)).astype(BF16)
+        g = (gst[:, c] + one[64:]) * rows[kb, 1:2, c] * rows[come_b, 0:1, c]
+        gst[:, c] = g
+        gz[1 - now, :128, c], gz[1 - now, 128:, c] = halves(g)
 
     sums = dot_nt(prods[...], sel[...])
     vs[spanf, :] = sums[0:64] + sums[64:128]
     ws[spanb, :] = sums[128:192] + sums[192:256]
-
-    r1 = dot_nt(ll[...], zf[0:256, :])
-    r2 = dot_nt(ll[0:64, :], zf[256:384, :])
-    pair = r1[:64, 128:] + r1[64:, 128:]
-    pair = jnp.where(lower, pair, zero)
-    p_hi, p_lo = halves(pair)
-    grad_c = r1[:64, :128] + r1[64:, :128] + r2 + dot_nn(p_hi, b_ff) + dot_nn(p_lo, b_ff)
-    turned = jnp.transpose(pair)
-    t_hi, t_lo = halves(turned[:64] + turned[64:])
-    part[spanf, LANES:] = grad_c
-    part[spanf, :LANES] += dot_nn(t_hi, c_f) + dot_nn(t_lo, c_f)
-    r1 = dot_nt(xx[...], zb[0:128, :])
-    r2 = dot_nt(xx[0:64, :], zb[256:384, :])
-    part[spanb, :LANES] += r1[:64] + r1[64:] + r2
-
-    bt = jnp.transpose(b_ff.astype(F32)).astype(BF16)
-    ct = jnp.transpose(c_bb.astype(F32)).astype(BF16)
-    last = step == blocks - 1
-    for c in chunks:
-        come = jnp.where(last, 1.0, rows[jnp.minimum(kf + 1, blocks - 1), 1:2, c])
-        h = (hst[:, c] + dot_nn(bt, zf[128:256, c])) * rows[kf, 0:1, c] * come
-        hst[:, c] = h
-        zf[0:128, c], zf[256:384, c] = halves(h)
-        g = (gst[:, c] + dot_nn(ct, zb[128:256, c])) * rows[kb, 1:2, c] * rows[jnp.maximum(kb - 1, 0), 0:1, c]
-        gst[:, c] = g
-        zb[0:128, c], zb[256:384, c] = halves(g)
-
-    @pl.when(step == half)
+    r = dot_nt(hz[now], lf_ref[0])
+    turned = jnp.transpose(r[:128] + r[128:])
+    grad_c = part_ref[spanf, LANES:] + turned[:64] + turned[64:]
+    r = dot_nt(gz[now], xb_ref[0])
+    turned = jnp.transpose(r[:128] + r[128:])
+    grad_b = part_ref[spanb, :LANES] + turned[:64] + turned[64:]
+    stage[step, :, :lines] = grad_c.reshape(zs, lines, LANES)
+    stage[step, :, lines:] = grad_b.reshape(zs, lines, LANES)
+
+    @pl.when(step == 0)
     def _():
         pl.semaphore_wait(barrier, zs - 1 + flats - 1)
 
-    @pl.when(step >= half)
+    for d in range(1, zs):
+        scatter(step, d).start()
+
+    @pl.when(step >= 1)
     def _():
-        j = step - half
-        for q in range(zs):
-            stage[j, q, :lines] = part[pl.ds(pl.multiple_of(kf * Q + q * lines, lines), lines), :]
-            stage[j, q, lines:] = part[pl.ds(pl.multiple_of(kb * Q + q * lines, lines), lines), :]
-        for d in range(1, zs):
-            scatter(j, d).start()
-
-    @pl.when(step >= half + 1)
+        reduce_pair(step - 1)
+
+    @pl.when(step >= 2)
     def _():
-        reduce_pair(step - half - 1)
-
-    @pl.when(step >= half + 2)
-    def _():
-        finish_pair(step - half - 2)
+        finish_pair(step - 2)
 
     @pl.when(step == blocks - 1)
     def _():
         closing = jnp.concatenate(
             [jnp.sum(gin_ref[i] * hst[:, c], axis=0, keepdims=True) for i, c in enumerate(chunks)], axis=1)
-        totals = jnp.concatenate([closing, jnp.sum(yx[...], axis=0, keepdims=True), jnp.zeros((14, width), F32)], axis=0)
-        hi, lo = halves(totals)
+        hi, lo = halves(jnp.broadcast_to(closing, (16, width)))
         totals = dot_nt(hi, sel[...]) + dot_nt(lo, sel[...])
         after = totals[0:1]
         gdts = []
@@ -507,15 +556,15 @@
             gdts.append(grad_dt)
             d_alog = d_alog + jnp.sum(dlog * dt, axis=0, keepdims=True)
             d_bias = d_bias + jnp.sum(grad_dt, axis=0, keepdims=True)
-        hsum[...] = jnp.concatenate([d_alog * rate, d_bias, totals[1:2], jnp.zeros((5, LANES), F32)], axis=0)
+        hsum[...] = jnp.concatenate([d_alog * rate, d_bias, dskip_ref[0:1], jnp.zeros((5, LANES), F32)], axis=0)
 
         @pl.loop(1, flats)
         def _(d):
             share(d).start()
 
-        reduce_pair(half - 1)
+        reduce_pair(blocks - 1)
         gdt_ref[...] = jnp.transpose(jnp.concatenate(gdts[::-1], axis=0))[:heads]
-        finish_pair(half - 2)
+        finish_pair(blocks - 2)
         hgot[flat] = hsum[...]
 
         @pl.loop(1, flats)
@@ -525,24 +574,24 @@
         total = hgot[0]
         for other in range(1, flats):
             total = total + hgot[other]
-        gheads_ref[...] = total * scale
-        finish_pair(half - 1)
+        gheads_ref[...] = total[:3, :heads] * scale
+        finish_pair(blocks - 1)
 
         @pl.loop(1, flats)
         def _(d):
             share(d).wait_send()
 
-        @pl.loop(0, half)
+        @pl.loop(0, blocks)
         def _(j):
             for d in range(1, zs):
                 scatter(j, d).wait_send()
                 gather(j, d).wait_send()
 
 
-def main(x, y, bc, dt, bias, alog, skip, hin, gin):
-    length, width = x.shape
+def main(y, dt, bias, alog, skip, hin, gin, dskip, xs, ls, fs, af, ab, part):
+    length, width = y.shape
     heads = dt.shape[0]
-    state = bc.shape[1] // 2
+    state = hin.shape[1]
     blocks = length // Q
     zs, dps = lax.axis_size("head"), lax.axis_size("dp")
     flats = lax.axis_size("seq") * dps
@@ -550,8 +599,11 @@
     lines = Q // zs
     dma = pltpu.SemaphoreType.DMA
     whole = pl.BlockSpec(memory_space=pltpu.VMEM)
-    ahead = pl.BlockSpec((Q, width), lambda i: (i, 0))
     back = pl.BlockSpec((Q, width), lambda i: (blocks - 1 - i, 0))
+    pair_f = pl.BlockSpec((1, 2 * Q, width), lambda i: (i, 0, 0))
+    pair_b = pl.BlockSpec((1, 2 * Q, width), lambda i: (blocks - 1 - i, 0, 0))
+    left_f = pl.BlockSpec((1, 4 * Q, 4 * Q), lambda i: (i, 0, 0))
+    left_b = pl.BlockSpec((1, 4 * Q, 4 * Q), lambda i: (blocks - 1 - i, 0, 0))
     return pl.pallas_call(
         functools.partial(main_kernel, heads, zs, dps, flats, scale),
         grid=(blocks,),
@@ -559,50 +611,44 @@
             jax.ShapeDtypeStruct((length, width), BF16),
             jax.ShapeDtypeStruct((length, 2 * state), F32),
             jax.ShapeDtypeStruct((heads, length), F32),
-            jax.ShapeDtypeStruct((8, LANES), F32),
+            jax.ShapeDtypeStruct((3, heads), F32),
         ),
-        in_specs=[ahead, ahead, back, back] + [whole] * 7,
+        in_specs=[pair_f, pair_f, pair_b, pair_b, back, back, left_f, left_b] + [whole] * 8,
         out_specs=(back, whole, whole, whole),
         scratch_shapes=[
-            pltpu.VMEM((length, LANES), BF16),
-            pltpu.VMEM((length, LANES), BF16),
             pltpu.VMEM((length, LANES), F32),
             pltpu.VMEM((length, LANES), F32),
             pltpu.VMEM((LANES, width), BF16),
             pltpu.VMEM((blocks + 1, 8, width), F32),
             pltpu.VMEM((length, LANES), F32),
             pltpu.VMEM((length, LANES), F32),
-            pltpu.VMEM((384, width), BF16),
-            pltpu.VMEM((384, width), BF16),
-            pltpu.VMEM((128, width), BF16),
-            pltpu.VMEM((128, width), BF16),
+            pltpu.VMEM((2, 256, width), BF16),
+            pltpu.VMEM((2, 256, width), BF16),
             pltpu.VMEM((256, width), BF16),
             pltpu.VMEM((state, width), F32),
             pltpu.VMEM((state, width), F32),
-            pltpu.VMEM((8, width), F32),
-            pltpu.VMEM((length, 2 * state), F32),
-            pltpu.VMEM((blocks // 2, zs, 2 * lines, 2 * state), F32),
-            pltpu.VMEM((blocks // 2, zs, 2 * lines, 2 * state), F32),
-            pltpu.VMEM((blocks // 2, zs, 2 * lines, 2 * state), F32),
+            pltpu.VMEM((blocks, zs, 2 * lines, state), F32),
+            pltpu.VMEM((blocks, zs, 2 * lines, state), F32),
+            pltpu.VMEM((blocks, zs, 2 * lines, state), F32),
             pltpu.VMEM((8, LANES), F32),
             pltpu.VMEM((flats, 8, LANES), F32),
-            dma((blocks // 2, zs)), dma((blocks // 2, zs)),
-            dma((blocks // 2, zs)), dma((blocks // 2, zs)),
+            dma((blocks, zs)), dma((blocks, zs)),
+            dma((blocks, zs)), dma((blocks, zs)),
             dma((flats,)), dma((flats,)),
         ],
         compiler_params=pltpu.CompilerParams(
             vmem_limit_bytes=VMEM_LIMIT, collective_id=1, has_side_effects=True, dimension_semantics=("arbitrary",)),
         cost_estimate=pl.CostEstimate(flops=60 * length * width * state, bytes_accessed=12 * length * width, transcendentals=0),
-    )(x, y, x, y, bc, dt, bias, alog, skip, hin, gin)
+    )(xs, ls, xs, ls, fs, y, af, ab, part, dskip, dt, bias, alog, skip, hin, gin)
 
 
 def shards(inputs_x, inputs_bc, dt_raw, grad_out, a_log, dt_bias, skip):
     heads = a_log.shape[0]
     x, y, bc, dt = inputs_x[0], grad_out[0], inputs_bc[0], dt_raw[0].T
     bias, alog, skips = dt_bias[None], a_log[None], skip[None]
-    hin, gin = edges(x, y, bc, dt, bias, alog)
-    grad_x, grad_bc, grad_dt, sums = main(x, y, bc, dt, bias, alog, skips, hin, gin)
-    return (grad_x[None], grad_bc[None], grad_dt.T[None], sums[:3, :heads])
+    hin, gin, *prepared = edges(x, y, bc, dt, bias, alog)
+    grad_x, grad_bc, grad_dt, sums = main(y, dt, bias, alog, skips, hin, gin, *prepared)
+    return (grad_x[None], grad_bc[None], grad_dt.T[None], sums)
 
 
 def solution(mesh):

time: 143 us -> 128 us (0.90)
  Pallas kernels: 134 us -> 120 us
    pallas_call x1, Pallas kernels: 88.5 us -> 73.6 us  [main(): pl.pallas_call(functools.partial(main_kernel, heads, zs, dps, flats, scal...]
    unnamed x7 -> x10, local copies, waits for them, and re-layouts: 6.52 us -> 7.1 us
where the time goes in v3:
time: 128 us; the launch traced here: 127 us
  Pallas kernels  120 us (94%)
  local copies, waits for them, and re-layouts  7.1 us (6%)
    pallas_call x1, Pallas kernels, main(): pl.pallas_call(functools.partial(main_kernel, heads, zs, dps, flats, scal...  73.6 us
    pallas_call x1, Pallas kernels, edges(): pl.pallas_call(functools.partial(edges_kernel, heads), out_shape=(jax.Sha...  46.1 us
    unnamed x10, local copies, waits for them, and re-layouts  7.1 us

profile of v3, /device:TPU:0, one launch (start us, length us, event | category | flops | bytes accessed | tf_op | source)
XLA Modules:
  0.0 127.4 jit_solution(10897545015607723439)
XLA Ops:
  0.6 46.1 %shard_map.102 = (f32[8,128,256]{2,1,0:T(8,128)}, f32[8,128,256]{2,1,0:T(8,128)}, f32[8,128]{1,0:T(8,128)}, bf16[16,128,2048]{2,1,0:T(8,128)(2,1)}, bf16[16,128,...) custom-call(bf16[1024,2048]{1,0:T(8,128)(2,1)} %bitcast.14, ...), custom_call_target="tpu_custom_call" | custom-call | flops 2147483648 | bytes 8388608 | tf_op jit(solution)/shard_map/pallas_call | solution.py:312
  46.7 73.6 %shard_map.103 = (bf16[1024,2048]{1,0:T(8,128)(2,1)}, f32[1024,256]{1,0:T(8,128)}, f32[32,1024]{1,0:T(8,128)}, f32[3,32]{1,0:T(4,128)}) custom-call(bf16[16,128,2048]{2,1,0:T(8,128)(2,1)} %get-tuple-element.17.xf_ref.xb_ref, bf16[16,128,2048]{2,1,0:T(8,128)(2,1)} %get-tuple-element.18.lf_ref.lb_ref, bf16[16,128,2048]{2,1,0:T(8,128)(2,1)} %get-tuple-element.17.xf_ref.xb_ref, ...), custom_call_target="tpu_custom_call" | custom-call | flops 16106127360 | bytes 25165824 | tf_op jit(solution)/shard_map/pallas_call | solution.py:607
  120.3 0.0 copy-start
  120.3 0.0 copy-start.1
  120.3 0.0 copy-start.2
  120.3 4.9 %copy.15 = bf16[1,1024,2048]{2,1,0:T(8,128)(2,1)} copy(bf16[1,1024,2048]{2,1,0:T(8,128)(2,1)} %bitcast.17) | data formatting | bytes 8388608
  125.2 0.0 copy-done
  125.2 1.0 copy.16
  126.2 0.0 copy-done.1
  126.2 0.7 copy.17
  126.9 0.0 copy-done.2
  126.9 0.6 copy.18
Async XLA Ops:
  120.3 4.9 %copy-start = (f32[1024,256]{1,0:T(8,128)S(1)}, f32[1024,256]{1,0:T(8,128)}, u32[]{:S(2)}) copy-start(f32[1024,256]{1,0:T(8,128)} %get-tuple-element.27) | copy-start | bytes 3145732
  120.3 5.9 %copy-start.1 = (f32[32,1024]{1,0:T(8,128)S(1)}, f32[32,1024]{1,0:T(8,128)}, u32[]{:S(2)}) copy-start(f32[32,1024]{1,0:T(8,128)} %get-tuple-element.28) | copy-start | bytes 393220
  120.3 6.5 %copy-start.2 = (f32[3,32]{1,0:T(4,128)S(1)}, f32[3,32]{1,0:T(4,128)}, u32[]{:S(2)}) copy-start(f32[3,32]{1,0:T(4,128)} %get-tuple-element.37) | copy-start | bytes 1156

commit v4 on v3

--- a/solution.py
+++ b/solution.py
@@ -9,13 +9,14 @@
 from jax.sharding import PartitionSpec as P
 
 Q = 64
+LAG = 2
 CHUNK = 256
 HEADDIM = 64
 LANES = 128
 HIGH = lax.Precision.HIGHEST
 F32 = jnp.float32
 BF16 = jnp.bfloat16
-VMEM_LIMIT = 56 * 1024 * 1024
+VMEM_LIMIT = 60 * 1024 * 1024
 
 
 def dot_nn(a, b, precision=None):
@@ -70,19 +71,20 @@
     return -jnp.exp(repeat_heads(jnp.broadcast_to(alog_ref[...], (8, heads)), heads))[:1]
 
 
-def edges_kernel(heads, x_ref, y_ref, bc_ref, dt_ref, bias_ref, alog_ref,
-                 hin_ref, gin_ref, skip_ref, xo_ref, lo_ref, fo_ref, af_ref, ab_ref, part_ref,
-                 pe, pf, le, lf, bt, ct, sel, xb, yb, xs, ys, dec, mine, out0, got0, chip, gath, pre, inc, fin,
-                 xbuf, lbuf, fbuf, abuf, bbuf, part, yx,
+def edges_kernel(heads, x_ref, y_ref, bc_ref, dt_ref, bias_ref, alog_ref, weight_ref,
+                 gin_ref, hst, skip_ref, part, dts, shs, rows, vs, xo_ref, lo_ref, fo_ref, ab_ref,
+                 pe, pf, le, lf, bt, ct, sel, xb, yb, xs, dec, mine, out0, got0, chip, gath, pre, inc, fin,
+                 xbuf, lbuf, fbuf, abuf, bbuf, yx, hz, prods,
                  load_sem, s0, r0, s1, r1, s2, r2, s3, r3, put_sem, put_one):
     length = bc_ref.shape[0]
     blocks = length // Q
-    groups = hin_ref.shape[0]
-    state = hin_ref.shape[1]
+    groups = gin_ref.shape[0]
+    state = gin_ref.shape[1]
     me = lax.axis_index("seq")
     core = lax.rem(me, 2)
     place = me // 2
     ahead = core == 1
+    behind = core == 0
     partner = me + 1 - 2 * core
 
     def peer(d):
@@ -134,7 +136,10 @@
 
     sel[...] = head_lanes(heads, sel.shape[1])
     rate = rates_of(alog_ref, heads)
-    dt = jax.nn.softplus(steps_of(dt_ref, bias_ref, heads))
+    shifted = steps_of(dt_ref, bias_ref, heads)
+    shs[...] = shifted
+    dt = jax.nn.softplus(shifted)
+    dts[...] = dt
     tri = triangle(False)
     cums = [dot_nn(tri, dt[k * Q:(k + 1) * Q] * rate, HIGH) for k in range(blocks)]
     before = jnp.zeros((1, LANES), F32)
@@ -166,7 +171,10 @@
         if i < groups - 1:
             chip[i, :state, :] = value
             chip[i, state:, :] = decay
-            spread(i + 1).start()
+
+            @pl.when(ahead)
+            def _():
+                spread(i + 1).start()
         else:
             gath[place, :state, :] = value
             gath[place, state:, :] = decay
@@ -182,9 +190,9 @@
         ends = dot_nn(bt[...], xs[...])
         copy_y.wait()
         hi, lo = halves(dot_nn(pe[...], here) * yb[i].astype(F32))
-        ys[:length] = hi
-        ys[length:] = lo
-        starts = dot_nn(ct[...], ys[...])
+        xs[:length] = hi
+        xs[length:] = lo
+        starts = dot_nn(ct[...], xs[...])
         mine[i] = jnp.where(ahead, ends, starts)
         out0[i, :state, :] = jnp.where(ahead, starts, ends)
         out0[i, state:, :] = dot_nn(dec[...], here)
@@ -236,7 +244,23 @@
         for copy in puts(i):
             copy.start()
         if i == groups // 2:
-            scan()
+            pl.when(ahead)(scan)
+
+    def hand_all():
+        for d in range(groups):
+            g = peer(d)
+            if d:
+                back_in(g).wait_recv()
+            hand(g).start()
+
+    def spread_all():
+        for d in range(1, groups):
+            spread(d).start()
+
+    gone = jnp.concatenate([jnp.exp(cum[Q - 1:Q] - cum[Q // 2 - 1:Q // 2]) for cum in cums], axis=0)
+    come = jnp.concatenate([jnp.exp(cum[Q // 2 - 1:Q // 2]) for cum in cums], axis=0)
+    weights = repeat_heads(jnp.broadcast_to(weight_ref[...], (8, heads)), heads)
+    rows[...] = dot_nn(packed(jnp.concatenate([gone, come, weights], axis=0), heads, 3), sel[...])
 
     lane = iota((Q, 2 * Q), 1)
     row = iota((Q, 2 * Q), 0)
@@ -265,28 +289,86 @@
         t_hi, t_lo = halves(turned[:Q] + turned[Q:])
         part[span, :LANES] = dot_nn(t_hi, c) + dot_nn(t_lo, c)
 
-    put_all = (pltpu.make_async_copy(abuf, af_ref, put_one.at[0]),
-               pltpu.make_async_copy(bbuf, ab_ref, put_one.at[1]),
-               pltpu.make_async_copy(part, part_ref, put_one.at[2]))
-    for copy in put_all:
-        copy.start()
+        @pl.when((k == blocks // 4) & behind)
+        def _():
+            spread_all()
+
+        @pl.when((k == blocks // 2) & ahead)
+        def _():
+            hand_all()
+
+    put_ab = pltpu.make_async_copy(bbuf, ab_ref, put_one)
+    put_ab.start()
     sums = jnp.sum(yx[...], axis=0, keepdims=True)
     hi, lo = halves(jnp.broadcast_to(sums, yx.shape))
     skip_ref[...] = dot_nt(hi, sel[...]) + dot_nt(lo, sel[...])
 
-    for d in range(groups):
-        g = peer(d)
-        if d:
-            back_in(g).wait_recv()
-        hand(g).start()
-    for d in range(groups):
+    def own(d):
         g = peer(d)
         i = (d - 1) % groups
-        own = got0[i, state:state + 1, :] * inc[g] + got0[i, :state, :]
-        hand(g).wait_recv()
-        other = fin[g]
-        hin_ref[g] = jnp.where(ahead, own, other)
-        gin_ref[g] = jnp.where(ahead, other, own)
+        return got0[i, state:state + 1, :] * inc[g] + got0[i, :state, :]
+
+    def lanes_of(d):
+        return pl.ds(pl.multiple_of(peer(d) * CHUNK, CHUNK), CHUNK)
+
+    @pl.when(ahead)
+    def _():
+        for d in range(groups):
+            hst[:, lanes_of(d)] = own(d)
+
+    @pl.when(behind)
+    def _():
+        for d in range(groups):
+            hand(peer(d)).wait_recv()
+            hst[:, lanes_of(d)] = fin[peer(d)]
+
+    chunks = [slice(c * CHUNK, (c + 1) * CHUNK) for c in range(groups)]
+    for c in chunks:
+        h = hst[:, c] * rows[blocks:blocks + 1, c]
+        hst[:, c] = h
+        hz[0, :128, c], hz[0, 128:, c] = halves(h)
+
+    @pl.loop(0, blocks)
+    def _(k):
+        span = pl.ds(pl.multiple_of(k * Q, Q), Q)
+        now = lax.rem(k, 2)
+        first, second = abuf[k, :192], abuf[k, 192:]
+        come = blocks + jnp.minimum(k + 1, blocks - 1)
+        for c in chunks:
+            wide = xbuf[k, :, c]
+            one = dot_nn(first, jnp.concatenate([hz[now, :128, c], wide], axis=0))
+            two = dot_nn(second, jnp.concatenate([wide, hz[now, 128:, c]], axis=0))
+            lifted = lbuf[k, 64:, c].astype(F32) + lbuf[k, :64, c].astype(F32)
+            prods[0:64, c], prods[64:128, c] = halves(lifted * (one[:64] + two))
+            h = (hst[:, c] + one[64:]) * rows[pl.ds(k, 1), c]
+            h = h * jnp.where(k == blocks - 1, 1.0, rows[pl.ds(come, 1), c])
+            hst[:, c] = h
+            hz[1 - now, :128, c], hz[1 - now, 128:, c] = halves(h)
+        sums = dot_nt(prods[...], sel[...])
+        vs[span, :] = sums[0:64] + sums[64:128]
+        r = dot_nt(hz[now], lbuf[k])
+        turned = jnp.transpose(r[:128] + r[128:])
+        part[span, LANES:] += turned[:64] + turned[64:]
+
+        @pl.when((k == blocks // 4) & behind)
+        def _():
+            scan()
+
+        @pl.when((k == 3 * blocks // 4) & behind)
+        def _():
+            hand_all()
+
+    @pl.when(ahead)
+    def _():
+        for d in range(groups):
+            hand(peer(d)).wait_recv()
+            gin_ref[peer(d)] = fin[peer(d)]
+
+    @pl.when(behind)
+    def _():
+        for d in range(groups):
+            gin_ref[peer(d)] = own(d)
+
     for i in range(groups):
         swap(i).wait_send()
         hand(i).wait_send()
@@ -296,11 +378,10 @@
     for i in range(groups):
         for copy in puts(i):
             copy.wait()
-    for copy in put_all:
-        copy.wait()
-
-
-def edges(x, y, bc, dt, bias, alog):
+    put_ab.wait()
+
+
+def edges(x, y, bc, dt, bias, alog, skip):
     length, width = x.shape
     heads = dt.shape[0]
     state = bc.shape[1] // 2
@@ -313,17 +394,20 @@
         functools.partial(edges_kernel, heads),
         out_shape=(
             jax.ShapeDtypeStruct((groups, state, CHUNK), F32),
-            jax.ShapeDtypeStruct((groups, state, CHUNK), F32),
+            jax.ShapeDtypeStruct((state, width), F32),
             jax.ShapeDtypeStruct((8, LANES), F32),
+            jax.ShapeDtypeStruct((length, 2 * state), F32),
+            jax.ShapeDtypeStruct((length, LANES), F32),
+            jax.ShapeDtypeStruct((length, LANES), F32),
+            jax.ShapeDtypeStruct((2 * blocks + 8, width), F32),
+            jax.ShapeDtypeStruct((length, LANES), F32),
             jax.ShapeDtypeStruct((blocks, 2 * Q, width), BF16),
             jax.ShapeDtypeStruct((blocks, 2 * Q, width), BF16),
             jax.ShapeDtypeStruct((length, width), F32),
             jax.ShapeDtypeStruct((blocks, 4 * Q, 4 * Q), BF16),
-            jax.ShapeDtypeStruct((blocks, 4 * Q, 4 * Q), BF16),
-            jax.ShapeDtypeStruct((length, 2 * state), F32),
         ),
-        in_specs=[anywhere, anywhere, whole, whole, whole, whole],
-        out_specs=(whole, whole, whole) + (anywhere,) * 6,
+        in_specs=[anywhere, anywhere] + [whole] * 5,
+        out_specs=(whole,) * 8 + (anywhere,) * 4,
         scratch_shapes=[
             pltpu.VMEM((length, LANES), BF16),
             pltpu.VMEM((length, LANES), BF16),
@@ -334,7 +418,6 @@
             pltpu.VMEM((LANES, width), BF16),
             pltpu.VMEM((groups, length, CHUNK), BF16),
             pltpu.VMEM((groups, length, CHUNK), BF16),
-            pltpu.VMEM((2 * length, CHUNK), BF16),
             pltpu.VMEM((2 * length, CHUNK), BF16),
             pltpu.VMEM((8, LANES), BF16),
             pltpu.VMEM((groups, state, CHUNK), F32),
@@ -350,30 +433,30 @@
             pltpu.VMEM((length, width), F32),
             pltpu.VMEM((blocks, 4 * Q, 4 * Q), BF16),
             pltpu.VMEM((blocks, 4 * Q, 4 * Q), BF16),
-            pltpu.VMEM((length, 2 * state), F32),
             pltpu.VMEM((8, width), F32),
+            pltpu.VMEM((2, 256, width), BF16),
+            pltpu.VMEM((128, width), BF16),
             dma((2, groups)),
             dma((groups,)), dma((groups,)),
             dma((groups,)), dma((groups,)),
             dma((groups,)), dma((groups,)),
             dma((groups,)), dma((groups,)),
-            dma((3, groups)), dma((3,)),
+            dma((3, groups)), dma,
         ],
         compiler_params=pltpu.CompilerParams(vmem_limit_bytes=VMEM_LIMIT, collective_id=0, has_side_effects=True),
         cost_estimate=pl.CostEstimate(flops=8 * length * width * state, bytes_accessed=4 * length * width, transcendentals=0),
-    )(x, y, bc, dt, bias, alog)
-
-
-def main_kernel(heads, zs, dps, flats, scale, xf_ref, lf_ref, xb_ref, lb_ref, fb_ref, yb_ref, af_ref, ab_ref,
-                part_ref, dskip_ref, dt_ref, bias_ref, alog_ref, skip_ref, hin_ref, gin_ref,
+    )(x, y, bc, dt, bias, alog, skip)
+
+
+def main_kernel(heads, zs, dps, flats, scale, xb_ref, lb_ref, fb_ref, yb_ref, ab_ref,
+                gin_ref, hend_ref, dskip_ref, part_ref, dts, shs, rows, vs, alog_ref,
                 gx_ref, gbc_ref, gdt_ref, gheads_ref,
-                dts, shs, sel, rows, vs, ws, hz, gz, prods, hst, gst,
+                sel, ws, gz, prods, gst,
                 stage, landed, done, hsum, hgot, s1, r1s, s2, r2s, s3, r3s):
     length = dts.shape[0]
     width = sel.shape[1]
     blocks = length // Q
     step = pl.program_id(0)
-    kf = step
     kb = blocks - 1 - step
     chunks = [slice(c * CHUNK, (c + 1) * CHUNK) for c in range(width // CHUNK)]
     rate = rates_of(alog_ref, heads)
@@ -439,7 +522,7 @@
         for d in range(1, zs):
             gather_in(j, d).wait_recv()
         for q in range(zs):
-            gbc_ref[pl.ds(pl.multiple_of(j * Q + q * lines, lines), lines), LANES:] = done[j, q, :lines]
+            gbc_ref[pl.ds(pl.multiple_of((blocks - 1 - j) * Q + q * lines, lines), lines), LANES:] = done[j, q, :lines]
             gbc_ref[pl.ds(pl.multiple_of((blocks - 1 - j) * Q + q * lines, lines), lines), :LANES] = done[j, q, lines:]
 
     @pl.when(step == 0)
@@ -452,71 +535,33 @@
             pl.semaphore_signal(barrier, inc=1, device_id=fpeer(d), device_id_type=pl.DeviceIdType.MESH)
 
         sel[...] = head_lanes(heads, width)
-        shifted = steps_of(dt_ref, bias_ref, heads)
-        shs[...] = shifted
-        dt = jax.nn.softplus(shifted)
-        dts[...] = dt
-        tri = triangle(False)
-        mids, lasts = [], []
-        for k in range(blocks):
-            here = dt[k * Q:(k + 1) * Q]
-            cum = dot_nn(tri, here * rate, HIGH)
-            mid = cum[Q // 2 - 1:Q // 2]
-            mids.append(mid)
-            lasts.append(cum[Q - 1:Q])
-        for k in range(blocks):
-            gone = jnp.broadcast_to(jnp.exp(lasts[k] - mids[k]), (8, LANES))
-            come = jnp.broadcast_to(jnp.exp(mids[k]), (8, LANES))
-            factor = packed(jnp.where(iota((8, LANES), 0) == 0, gone, come), heads, 3)
-            rows[k] = dot_nn(factor, sel[...])
-        skips = repeat_heads(jnp.broadcast_to(skip_ref[...], (8, heads)), heads)
-        rows[blocks] = dot_nn(packed(skips, heads, 3), sel[...])
         for i, c in enumerate(chunks):
-            h = hin_ref[i] * rows[0, 1:2, c]
-            hst[:, c] = h
-            hz[0, :128, c], hz[0, 128:, c] = halves(h)
-            g = gin_ref[i] * rows[blocks - 1, 0:1, c]
+            g = gin_ref[i] * rows[blocks - 1:blocks, c]
             gst[:, c] = g
             gz[0, :128, c], gz[0, 128:, c] = halves(g)
 
-    spanf = pl.ds(pl.multiple_of(kf * Q, Q), Q)
-    spanb = pl.ds(pl.multiple_of(kb * Q, Q), Q)
+    span = pl.ds(pl.multiple_of(kb * Q, Q), Q)
     now = lax.rem(step, 2)
-    first_f, second_f = af_ref[0, :192], af_ref[0, 192:]
-    first_b, second_b = ab_ref[0, :192], ab_ref[0, 192:]
-    come_f = jnp.minimum(kf + 1, blocks - 1)
-    come_b = jnp.maximum(kb - 1, 0)
-    last = step == blocks - 1
+    first, second = ab_ref[0, :192], ab_ref[0, 192:]
+    come = jnp.maximum(kb - 1, 0)
     for c in chunks:
-        wide = xf_ref[0, :, c]
-        one = dot_nn(first_f, jnp.concatenate([hz[now, :128, c], wide], axis=0))
-        two = dot_nn(second_f, jnp.concatenate([wide, hz[now, 128:, c]], axis=0))
-        lifted = lf_ref[0, 64:, c].astype(F32) + lf_ref[0, :64, c].astype(F32)
-        prods[0:64, c], prods[64:128, c] = halves(lifted * (one[:64] + two))
-        h = (hst[:, c] + one[64:]) * rows[kf, 0:1, c] * jnp.where(last, 1.0, rows[come_f, 1:2, c])
-        hst[:, c] = h
-        hz[1 - now, :128, c], hz[1 - now, 128:, c] = halves(h)
-
         wide = lb_ref[0, :, c]
-        one = dot_nn(first_b, jnp.concatenate([gz[now, :128, c], wide], axis=0))
-        two = dot_nn(second_b, jnp.concatenate([wide, gz[now, 128:, c]], axis=0))
+        one = dot_nn(first, jnp.concatenate([gz[now, :128, c], wide], axis=0))
+        two = dot_nn(second, jnp.concatenate([wide, gz[now, 128:, c]], axis=0))
         out = one[:64] + two
         xs = xb_ref[0, 64:, c].astype(F32) + xb_ref[0, :64, c].astype(F32)
-        prods[128:192, c], prods[192:256, c] = halves(xs * out)
-        gx_ref[:, c] = (fb_ref[:, c] * out + rows[blocks, :1, c] * yb_ref[:, c].astype(F32)).astype(BF16)
-        g = (gst[:, c] + one[64:]) * rows[kb, 1:2, c] * rows[come_b, 0:1, c]
+        prods[0:64, c], prods[64:128, c] = halves(xs * out)
+        gx_ref[:, c] = (fb_ref[:, c] * out + rows[2 * blocks:2 * blocks + 1, c] * yb_ref[:, c].astype(F32)).astype(BF16)
+        g = (gst[:, c] + one[64:]) * rows[pl.ds(blocks + kb, 1), c] * rows[pl.ds(come, 1), c]
         gst[:, c] = g
         gz[1 - now, :128, c], gz[1 - now, 128:, c] = halves(g)
 
     sums = dot_nt(prods[...], sel[...])
-    vs[spanf, :] = sums[0:64] + sums[64:128]
-    ws[spanb, :] = sums[128:192] + sums[192:256]
-    r = dot_nt(hz[now], lf_ref[0])
-    turned = jnp.transpose(r[:128] + r[128:])
-    grad_c = part_ref[spanf, LANES:] + turned[:64] + turned[64:]
+    ws[span, :] = sums[0:64] + sums[64:128]
     r = dot_nt(gz[now], xb_ref[0])
     turned = jnp.transpose(r[:128] + r[128:])
-    grad_b = part_ref[spanb, :LANES] + turned[:64] + turned[64:]
+    grad_b = part_ref[span, :LANES] + turned[:64] + turned[64:]
+    grad_c = part_ref[span, LANES:]
     stage[step, :, :lines] = grad_c.reshape(zs, lines, LANES)
     stage[step, :, lines:] = grad_b.reshape(zs, lines, LANES)
 
@@ -527,18 +572,18 @@
     for d in range(1, zs):
         scatter(step, d).start()
 
-    @pl.when(step >= 1)
-    def _():
-        reduce_pair(step - 1)
-
-    @pl.when(step >= 2)
-    def _():
-        finish_pair(step - 2)
+    @pl.when(step >= LAG)
+    def _():
+        reduce_pair(step - LAG)
+
+    @pl.when(step >= 2 * LAG)
+    def _():
+        finish_pair(step - 2 * LAG)
 
     @pl.when(step == blocks - 1)
     def _():
         closing = jnp.concatenate(
-            [jnp.sum(gin_ref[i] * hst[:, c], axis=0, keepdims=True) for i, c in enumerate(chunks)], axis=1)
+            [jnp.sum(gin_ref[i] * hend_ref[:, c], axis=0, keepdims=True) for i, c in enumerate(chunks)], axis=1)
         hi, lo = halves(jnp.broadcast_to(closing, (16, width)))
         totals = dot_nt(hi, sel[...]) + dot_nt(lo, sel[...])
         after = totals[0:1]
@@ -562,9 +607,11 @@
         def _(d):
             share(d).start()
 
-        reduce_pair(blocks - 1)
+        for j in range(blocks - LAG, blocks):
+            reduce_pair(j)
         gdt_ref[...] = jnp.transpose(jnp.concatenate(gdts[::-1], axis=0))[:heads]
-        finish_pair(blocks - 2)
+        for j in range(blocks - 2 * LAG, blocks - LAG):
+            finish_pair(j)
         hgot[flat] = hsum[...]
 
         @pl.loop(1, flats)
@@ -575,7 +622,8 @@
         for other in range(1, flats):
             total = total + hgot[other]
         gheads_ref[...] = total[:3, :heads] * scale
-        finish_pair(blocks - 1)
+        for j in range(blocks - LAG, blocks):
+            finish_pair(j)
 
         @pl.loop(1, flats)
         def _(d):
@@ -588,10 +636,9 @@
                 gather(j, d).wait_send()
 
 
-def main(y, dt, bias, alog, skip, hin, gin, dskip, xs, ls, fs, af, ab, part):
+def main(heads, y, alog, gin, hend, dskip, part, dts, shs, rows, vs, xs, ls, fs, ab):
     length, width = y.shape
-    heads = dt.shape[0]
-    state = hin.shape[1]
+    state = gin.shape[1]
     blocks = length // Q
     zs, dps = lax.axis_size("head"), lax.axis_size("dp")
     flats = lax.axis_size("seq") * dps
@@ -600,9 +647,7 @@
     dma = pltpu.SemaphoreType.DMA
     whole = pl.BlockSpec(memory_space=pltpu.VMEM)
     back = pl.BlockSpec((Q, width), lambda i: (blocks - 1 - i, 0))
-    pair_f = pl.BlockSpec((1, 2 * Q, width), lambda i: (i, 0, 0))
     pair_b = pl.BlockSpec((1, 2 * Q, width), lambda i: (blocks - 1 - i, 0, 0))
-    left_f = pl.BlockSpec((1, 4 * Q, 4 * Q), lambda i: (i, 0, 0))
     left_b = pl.BlockSpec((1, 4 * Q, 4 * Q), lambda i: (blocks - 1 - i, 0, 0))
     return pl.pallas_call(
         functools.partial(main_kernel, heads, zs, dps, flats, scale),
@@ -613,19 +658,13 @@
             jax.ShapeDtypeStruct((heads, length), F32),
             jax.ShapeDtypeStruct((3, heads), F32),
         ),
-        in_specs=[pair_f, pair_f, pair_b, pair_b, back, back, left_f, left_b] + [whole] * 8,
+        in_specs=[pair_b, pair_b, back, back, left_b] + [whole] * 9,
         out_specs=(back, whole, whole, whole),
         scratch_shapes=[
-            pltpu.VMEM((length, LANES), F32),
-            pltpu.VMEM((length, LANES), F32),
             pltpu.VMEM((LANES, width), BF16),
-            pltpu.VMEM((blocks + 1, 8, width), F32),
-            pltpu.VMEM((length, LANES), F32),
             pltpu.VMEM((length, LANES), F32),
             pltpu.VMEM((2, 256, width), BF16),
-            pltpu.VMEM((2, 256, width), BF16),
-            pltpu.VMEM((256, width), BF16),
-            pltpu.VMEM((state, width), F32),
+            pltpu.VMEM((128, width), BF16),
             pltpu.VMEM((state, width), F32),
             pltpu.VMEM((blocks, zs, 2 * lines, state), F32),
             pltpu.VMEM((blocks, zs, 2 * lines, state), F32),
@@ -639,15 +678,15 @@
         compiler_params=pltpu.CompilerParams(
             vmem_limit_bytes=VMEM_LIMIT, collective_id=1, has_side_effects=True, dimension_semantics=("arbitrary",)),
         cost_estimate=pl.CostEstimate(flops=60 * length * width * state, bytes_accessed=12 * length * width, transcendentals=0),
-    )(xs, ls, xs, ls, fs, y, af, ab, part, dskip, dt, bias, alog, skip, hin, gin)
+    )(xs, ls, fs, y, ab, gin, hend, dskip, part, dts, shs, rows, vs, alog)
 
 
 def shards(inputs_x, inputs_bc, dt_raw, grad_out, a_log, dt_bias, skip):
     heads = a_log.shape[0]
     x, y, bc, dt = inputs_x[0], grad_out[0], inputs_bc[0], dt_raw[0].T
     bias, alog, skips = dt_bias[None], a_log[None], skip[None]
-    hin, gin, *prepared = edges(x, y, bc, dt, bias, alog)
-    grad_x, grad_bc, grad_dt, sums = main(y, dt, bias, alog, skips, hin, gin, *prepared)
+    prepared = edges(x, y, bc, dt, bias, alog, skips)
+    grad_x, grad_bc, grad_dt, sums = main(heads, y, alog, *prepared)
     return (grad_x[None], grad_bc[None], grad_dt.T[None], sums)
 
 

time: 128 us -> 120 us (0.938)
  Pallas kernels: 120 us -> 112 us
    pallas_call x1, Pallas kernels: 73.6 us -> 51.6 us  [main(): pl.pallas_call(functools.partial(main_kernel, heads, zs, dps, flats, scal...]
    pallas_call x1, Pallas kernels: 46.1 us -> 60.5 us  [edges(): pl.pallas_call(functools.partial(edges_kernel, heads), out_shape=(jax.Sha...]
where the time goes in v4:
time: 120 us
  Pallas kernels  112 us (93%)
  local copies, waits for them, and re-layouts  7.1 us (6%)
    pallas_call x1, Pallas kernels, edges(): pl.pallas_call(functools.partial(edges_kernel, heads), out_shape=(jax.Sha...  60.5 us
    pallas_call x1, Pallas kernels, main(): pl.pallas_call(functools.partial(main_kernel, heads, zs, dps, flats, scal...  51.6 us
    unnamed x10, local copies, waits for them, and re-layouts  7.1 us

profile of v4, /device:TPU:0, one launch (start us, length us, event | category | flops | bytes accessed | tf_op | source)
XLA Modules:
  0.0 119.9 jit_solution(5507915957729923589)
XLA Ops:
  0.6 60.5 %shard_map.102 = (f32[8,128,256]{2,1,0:T(8,128)}, f32[128,2048]{1,0:T(8,128)}, f32[8,128]{1,0:T(8,128)}, f32[1024,256]{1,0:T(8,128)}, f32[1024,128]{1,0:T(8,128)...) custom-call(bf16[1024,2048]{1,0:T(8,128)(2,1)} %bitcast.14, ...), custom_call_target="tpu_custom_call" | custom-call | flops 2147483648 | bytes 8388608 | tf_op jit(solution)/shard_map/pallas_call | solution.py:393
  61.1 51.6 %shard_map.103 = (bf16[1024,2048]{1,0:T(8,128)(2,1)}, f32[1024,256]{1,0:T(8,128)}, f32[32,1024]{1,0:T(8,128)}, f32[3,32]{1,0:T(4,128)}) custom-call(bf16[16,128,2048]{2,1,0:T(8,128)(2,1)} %get-tuple-element.20.xb_ref, bf16[16,128,2048]{2,1,0:T(8,128)(2,1)} %get-tuple-element.21.lb_ref, f32[1024,2048]{1,0:T(8,128)} %get-tuple-element.22.fb_ref, ...), custom_call_target="tpu_custom_call" | custom-call | flops 16106127360 | bytes 25165824 | tf_op jit(solution)/shard_map/pallas_call | solution.py:652
  112.7 0.0 copy-start
  112.7 0.0 copy-start.1
  112.8 0.0 copy-start.2
  112.8 4.9 %copy.15 = bf16[1,1024,2048]{2,1,0:T(8,128)(2,1)} copy(bf16[1,1024,2048]{2,1,0:T(8,128)(2,1)} %bitcast.17) | data formatting | bytes 8388608
  117.6 0.0 copy-done
  117.6 1.0 copy.16
  118.6 0.0 copy-done.1
  118.6 0.7 copy.17
  119.3 0.0 copy-done.2
  119.3 0.6 copy.18
Async XLA Ops:
  112.7 4.9 %copy-start = (f32[1024,256]{1,0:T(8,128)S(1)}, f32[1024,256]{1,0:T(8,128)}, u32[]{:S(2)}) copy-start(f32[1024,256]{1,0:T(8,128)} %get-tuple-element.33) | copy-start | bytes 3145732
  112.7 5.9 %copy-start.1 = (f32[32,1024]{1,0:T(8,128)S(1)}, f32[32,1024]{1,0:T(8,128)}, u32[]{:S(2)}) copy-start(f32[32,1024]{1,0:T(8,128)} %get-tuple-element.34) | copy-start | bytes 393220
  112.8 6.5 %copy-start.2 = (f32[3,32]{1,0:T(4,128)S(1)}, f32[3,32]{1,0:T(4,128)}, u32[]{:S(2)}) copy-start(f32[3,32]{1,0:T(4,128)} %get-tuple-element.43) | copy-start | bytes 1156

commit v5 on v4

--- a/solution.py
+++ b/solution.py
@@ -9,7 +9,7 @@
 from jax.sharding import PartitionSpec as P
 
 Q = 64
-LAG = 2
+LAG = 3
 CHUNK = 256
 HEADDIM = 64
 LANES = 128
@@ -71,11 +71,76 @@
     return -jnp.exp(repeat_heads(jnp.broadcast_to(alog_ref[...], (8, heads)), heads))[:1]
 
 
+class HeadSum:
+    def __init__(self, stage, landed, done, sems):
+        self.stage, self.landed, self.done = stage, landed, done
+        self.s1, self.r1, self.s2, self.r2 = sems
+        self.zs, self.z = stage.shape[1], lax.axis_index("head")
+
+    def peer(self, d):
+        return lax.rem(self.z + d, self.zs)
+
+    def copy(self, src, dst, send, recv, q):
+        return pltpu.make_async_remote_copy(
+            src_ref=src, dst_ref=dst, send_sem=send, recv_sem=recv,
+            device_id={"head": q}, device_id_type=pl.DeviceIdType.MESH)
+
+    def scatter(self, j, d):
+        q = self.peer(d)
+        return self.copy(self.stage.at[j, q], self.landed.at[j, self.z], self.s1.at[j, q], self.r1.at[j, self.z], q)
+
+    def gather(self, j, d):
+        q = self.peer(d)
+        return self.copy(self.done.at[j, self.z], self.done.at[j, self.z], self.s2.at[j, q], self.r2.at[j, self.z], q)
+
+    def send(self, j, value):
+        self.stage[j] = value.reshape(self.stage.shape[1:])
+        for d in range(1, self.zs):
+            self.scatter(j, d).start()
+
+    def reduce(self, j):
+        for d in range(1, self.zs):
+            q = self.peer(d)
+            self.copy(self.stage.at[j, q], self.landed.at[j, q], self.s1.at[j, q], self.r1.at[j, q], q).wait_recv()
+        self.landed[j, self.z] = self.stage[j, self.z]
+        total = self.landed[j, 0]
+        for q in range(1, self.zs):
+            total = total + self.landed[j, q]
+        self.done[j, self.z] = total
+        for d in range(1, self.zs):
+            self.gather(j, d).start()
+
+    def result(self, j):
+        for d in range(1, self.zs):
+            q = self.peer(d)
+            self.copy(self.done.at[j, q], self.done.at[j, q], self.s2.at[j, q], self.r2.at[j, q], q).wait_recv()
+        return self.done[j].reshape(Q, LANES)
+
+    def sent(self):
+        @pl.loop(0, self.stage.shape[0])
+        def _(j):
+            for d in range(1, self.zs):
+                self.scatter(j, d).wait_send()
+                self.gather(j, d).wait_send()
+
+
+def head_sum_scratch(count, zs):
+    buffer = pltpu.VMEM((count, zs, Q // zs, LANES), F32)
+    return [buffer] * 3 + [pltpu.SemaphoreType.DMA((count, zs))] * 4
+
+
+def greet_heads(barrier, zs):
+    for d in range(1, zs):
+        pl.semaphore_signal(barrier, inc=1, device_id={"head": lax.rem(lax.axis_index("head") + d, zs)},
+                            device_id_type=pl.DeviceIdType.MESH)
+
+
 def edges_kernel(heads, x_ref, y_ref, bc_ref, dt_ref, bias_ref, alog_ref, weight_ref,
                  gin_ref, hst, skip_ref, part, dts, shs, rows, vs, xo_ref, lo_ref, fo_ref, ab_ref,
-                 pe, pf, le, lf, bt, ct, sel, xb, yb, xs, dec, mine, out0, got0, chip, gath, pre, inc, fin,
-                 xbuf, lbuf, fbuf, abuf, bbuf, yx, hz, prods,
-                 load_sem, s0, r0, s1, r1, s2, r2, s3, r3, put_sem, put_one):
+                 pe, pf, le, lf, bt, ct, sel, xb, yb, xs, dec, out0, got0, chip, gath, pre, inc, fin,
+                 xbuf, lbuf, fbuf, abuf, bbuf, yx, hz,
+                 load_sem, s0, r0, s1, r1, s2, r2, s3, r3, put_sem, put_one,
+                 stage, landed, done, z1, z2, z3, z4):
     length = bc_ref.shape[0]
     blocks = length // Q
     groups = gin_ref.shape[0]
@@ -129,7 +194,10 @@
     for i in range(groups):
         for copy in loads(i):
             copy.start()
+    total_c = HeadSum(stage, landed, done, (z1, z2, z3, z4))
+    early = stage.shape[0]
     barrier = pltpu.get_barrier_semaphore()
+    greet_heads(barrier, total_c.zs)
     pl.semaphore_signal(barrier, inc=1, device_id={"seq": partner}, device_id_type=pl.DeviceIdType.MESH)
     for d in range(1, groups):
         pl.semaphore_signal(barrier, inc=1, device_id={"seq": peer(d) * 2 + core}, device_id_type=pl.DeviceIdType.MESH)
@@ -161,12 +229,12 @@
     bt[:, length:] = b_t
     ct[:, :length] = c_t
     ct[:, length:] = c_t
-    pl.semaphore_wait(barrier, groups)
+    pl.semaphore_wait(barrier, groups + total_c.zs - 1)
 
     def combine(i):
         swap(i).wait_recv()
         keep = out0[i, state:state + 1, :]
-        value = mine[i] + keep * got0[i, :state, :]
+        value = pre[i] + keep * got0[i, :state, :]
         decay = out0[i, state:, :] * got0[i, state:, :]
         if i < groups - 1:
             chip[i, :state, :] = value
@@ -193,7 +261,7 @@
         xs[:length] = hi
         xs[length:] = lo
         starts = dot_nn(ct[...], xs[...])
-        mine[i] = jnp.where(ahead, ends, starts)
+        pre[i] = jnp.where(ahead, ends, starts)
         out0[i, :state, :] = jnp.where(ahead, starts, ends)
         out0[i, state:, :] = dot_nn(dec[...], here)
         swap(i).start()
@@ -339,16 +407,30 @@
             one = dot_nn(first, jnp.concatenate([hz[now, :128, c], wide], axis=0))
             two = dot_nn(second, jnp.concatenate([wide, hz[now, 128:, c]], axis=0))
             lifted = lbuf[k, 64:, c].astype(F32) + lbuf[k, :64, c].astype(F32)
-            prods[0:64, c], prods[64:128, c] = halves(lifted * (one[:64] + two))
+            bt[0:64, c], bt[64:128, c] = halves(lifted * (one[:64] + two))
             h = (hst[:, c] + one[64:]) * rows[pl.ds(k, 1), c]
             h = h * jnp.where(k == blocks - 1, 1.0, rows[pl.ds(come, 1), c])
             hst[:, c] = h
             hz[1 - now, :128, c], hz[1 - now, 128:, c] = halves(h)
-        sums = dot_nt(prods[...], sel[...])
+        sums = dot_nt(bt[...], sel[...])
         vs[span, :] = sums[0:64] + sums[64:128]
         r = dot_nt(hz[now], lbuf[k])
         turned = jnp.transpose(r[:128] + r[128:])
-        part[span, LANES:] += turned[:64] + turned[64:]
+        grad_c = part[span, LANES:] + turned[:64] + turned[64:]
+        part[span, LANES:] = grad_c
+
+        @pl.when(k < early)
+        def _():
+            total_c.send(k, grad_c)
+
+        @pl.when((k >= LAG) & (k < early + LAG))
+        def _():
+            total_c.reduce(k - LAG)
+
+        @pl.when(k >= 2 * LAG)
+        def _():
+            j = k - 2 * LAG
+            part[pl.ds(pl.multiple_of(j * Q, Q), Q), LANES:] = total_c.result(j)
 
         @pl.when((k == blocks // 4) & behind)
         def _():
@@ -379,6 +461,7 @@
         for copy in puts(i):
             copy.wait()
     put_ab.wait()
+    total_c.sent()
 
 
 def edges(x, y, bc, dt, bias, alog, skip):
@@ -420,7 +503,6 @@
             pltpu.VMEM((groups, length, CHUNK), BF16),
             pltpu.VMEM((2 * length, CHUNK), BF16),
             pltpu.VMEM((8, LANES), BF16),
-            pltpu.VMEM((groups, state, CHUNK), F32),
             pltpu.VMEM((groups, state + 8, CHUNK), F32),
             pltpu.VMEM((groups, state + 8, CHUNK), F32),
             pltpu.VMEM((groups - 1, state + 8, CHUNK), F32),
@@ -435,14 +517,13 @@
             pltpu.VMEM((blocks, 4 * Q, 4 * Q), BF16),
             pltpu.VMEM((8, width), F32),
             pltpu.VMEM((2, 256, width), BF16),
-            pltpu.VMEM((128, width), BF16),
             dma((2, groups)),
             dma((groups,)), dma((groups,)),
             dma((groups,)), dma((groups,)),
             dma((groups,)), dma((groups,)),
             dma((groups,)), dma((groups,)),
             dma((3, groups)), dma,
-        ],
+        ] + head_sum_scratch(blocks - 2 * LAG, lax.axis_size("head")),
         compiler_params=pltpu.CompilerParams(vmem_limit_bytes=VMEM_LIMIT, collective_id=0, has_side_effects=True),
         cost_estimate=pl.CostEstimate(flops=8 * length * width * state, bytes_accessed=4 * length * width, transcendentals=0),
     )(x, y, bc, dt, bias, alog, skip)
@@ -451,8 +532,8 @@
 def main_kernel(heads, zs, dps, flats, scale, xb_ref, lb_ref, fb_ref, yb_ref, ab_ref,
                 gin_ref, hend_ref, dskip_ref, part_ref, dts, shs, rows, vs, alog_ref,
                 gx_ref, gbc_ref, gdt_ref, gheads_ref,
-                sel, ws, gz, prods, gst,
-                stage, landed, done, hsum, hgot, s1, r1s, s2, r2s, s3, r3s):
+                sel, gdts, gz, prods, gst, carry, hsum, hgot, hmid, hall, s3, r3, s4, r4,
+                b_stage, b_landed, b_done, b1, b2, b3, b4, c_stage, c_landed, c_done, c1, c2, c3, c4):
     length = dts.shape[0]
     width = sel.shape[1]
     blocks = length // Q
@@ -460,85 +541,51 @@
     kb = blocks - 1 - step
     chunks = [slice(c * CHUNK, (c + 1) * CHUNK) for c in range(width // CHUNK)]
     rate = rates_of(alog_ref, heads)
-    lines = Q // zs
-    z = lax.axis_index("head")
+    total_b = HeadSum(b_stage, b_landed, b_done, (b1, b2, b3, b4))
+    total_c = HeadSum(c_stage, c_landed, c_done, (c1, c2, c3, c4))
+    late = c_stage.shape[0]
     flat = lax.axis_index("seq") * dps + lax.axis_index("dp")
+    near = hgot.shape[0]
+    far = hall.shape[0]
+    inner, outer = lax.rem(flat, near), flat // near
     barrier = pltpu.get_barrier_semaphore()
 
-    def zpeer(d):
-        return {"head": lax.rem(z + d, zs)}
-
-    def fpeer(d):
-        other = lax.rem(flat + d, flats)
-        return {"seq": other // dps, "dp": lax.rem(other, dps)}
-
-    def scatter(j, d):
-        q = lax.rem(z + d, zs)
-        return pltpu.make_async_remote_copy(
-            src_ref=stage.at[j, q], dst_ref=landed.at[j, z], send_sem=s1.at[j, q], recv_sem=r1s.at[j, z],
-            device_id=zpeer(d), device_id_type=pl.DeviceIdType.MESH)
-
-    def scatter_in(j, d):
-        q = lax.rem(z + d, zs)
-        return pltpu.make_async_remote_copy(
-            src_ref=stage.at[j, q], dst_ref=landed.at[j, q], send_sem=s1.at[j, q], recv_sem=r1s.at[j, q],
-            device_id=zpeer(d), device_id_type=pl.DeviceIdType.MESH)
-
-    def gather(j, d):
-        q = lax.rem(z + d, zs)
-        return pltpu.make_async_remote_copy(
-            src_ref=done.at[j, z], dst_ref=done.at[j, z], send_sem=s2.at[j, q], recv_sem=r2s.at[j, z],
-            device_id=zpeer(d), device_id_type=pl.DeviceIdType.MESH)
-
-    def gather_in(j, d):
-        q = lax.rem(z + d, zs)
-        return pltpu.make_async_remote_copy(
-            src_ref=done.at[j, q], dst_ref=done.at[j, q], send_sem=s2.at[j, q], recv_sem=r2s.at[j, q],
-            device_id=zpeer(d), device_id_type=pl.DeviceIdType.MESH)
-
-    def share(d):
-        return pltpu.make_async_remote_copy(
-            src_ref=hsum, dst_ref=hgot.at[flat], send_sem=s3.at[d], recv_sem=r3s.at[flat],
-            device_id=fpeer(d), device_id_type=pl.DeviceIdType.MESH)
-
-    def share_in(d):
-        other = lax.rem(flat + d, flats)
-        return pltpu.make_async_remote_copy(
-            src_ref=hsum, dst_ref=hgot.at[other], send_sem=s3.at[d], recv_sem=r3s.at[other],
-            device_id=fpeer(d), device_id_type=pl.DeviceIdType.MESH)
-
-    def reduce_pair(j):
-        for d in range(1, zs):
-            scatter_in(j, d).wait_recv()
-        landed[j, z] = stage[j, z]
-        total = landed[j, 0]
-        for q in range(1, zs):
-            total = total + landed[j, q]
-        done[j, z] = total
-        for d in range(1, zs):
-            gather(j, d).start()
-
-    def finish_pair(j):
-        for d in range(1, zs):
-            gather_in(j, d).wait_recv()
-        for q in range(zs):
-            gbc_ref[pl.ds(pl.multiple_of((blocks - 1 - j) * Q + q * lines, lines), lines), LANES:] = done[j, q, :lines]
-            gbc_ref[pl.ds(pl.multiple_of((blocks - 1 - j) * Q + q * lines, lines), lines), :LANES] = done[j, q, lines:]
+    def at(flat):
+        return {"seq": flat // dps, "dp": lax.rem(flat, dps)}
+
+    def share(d, source):
+        return pltpu.make_async_remote_copy(
+            src_ref=hsum, dst_ref=hgot.at[source], send_sem=s3.at[d], recv_sem=r3.at[source],
+            device_id=at(outer * near + lax.rem(inner + d, near)), device_id_type=pl.DeviceIdType.MESH)
+
+    def spread(d, source):
+        return pltpu.make_async_remote_copy(
+            src_ref=hmid, dst_ref=hall.at[source], send_sem=s4.at[d], recv_sem=r4.at[source],
+            device_id=at(lax.rem(outer + d, far) * near + inner), device_id_type=pl.DeviceIdType.MESH)
+
+    def rows_of(k):
+        return pl.ds(pl.multiple_of(k * Q, Q), Q)
 
     @pl.when(step == 0)
     def _():
-        for d in range(1, zs):
-            pl.semaphore_signal(barrier, inc=1, device_id=zpeer(d), device_id_type=pl.DeviceIdType.MESH)
-
-        @pl.loop(1, flats)
-        def _(d):
-            pl.semaphore_signal(barrier, inc=1, device_id=fpeer(d), device_id_type=pl.DeviceIdType.MESH)
-
+        greet_heads(barrier, zs)
+        for d in range(1, near):
+            pl.semaphore_signal(barrier, inc=1, device_id=at(outer * near + lax.rem(inner + d, near)),
+                                device_id_type=pl.DeviceIdType.MESH)
+        for d in range(1, far):
+            pl.semaphore_signal(barrier, inc=1, device_id=at(lax.rem(outer + d, far) * near + inner),
+                                device_id_type=pl.DeviceIdType.MESH)
         sel[...] = head_lanes(heads, width)
         for i, c in enumerate(chunks):
             g = gin_ref[i] * rows[blocks - 1:blocks, c]
             gst[:, c] = g
             gz[0, :128, c], gz[0, 128:, c] = halves(g)
+        closing = jnp.concatenate(
+            [jnp.sum(gin_ref[i] * hend_ref[:, c], axis=0, keepdims=True) for i, c in enumerate(chunks)], axis=1)
+        hi, lo = halves(jnp.broadcast_to(closing, (16, width)))
+        carry[...] = (dot_nt(hi, sel[...]) + dot_nt(lo, sel[...]))[:8]
+        hsum[...] = jnp.where(iota(hsum.shape, 0) == 2, dskip_ref[...], 0.0)
+        gbc_ref[:(blocks - late) * Q, LANES:] = part_ref[:(blocks - late) * Q, LANES:]
 
     span = pl.ds(pl.multiple_of(kb * Q, Q), Q)
     now = lax.rem(step, 2)
@@ -557,83 +604,80 @@
         gz[1 - now, :128, c], gz[1 - now, 128:, c] = halves(g)
 
     sums = dot_nt(prods[...], sel[...])
-    ws[span, :] = sums[0:64] + sums[64:128]
+    w = sums[0:64] + sums[64:128]
+    dt = dts[span, :]
+    dlog = dot_nn(triangle(True), vs[span, :] - w, HIGH) + carry[0:1]
+    carry[...] = jnp.broadcast_to(dlog[0:1], carry.shape)
+    grad_dt = (w / dt + dlog * rate) * jax.nn.sigmoid(shs[span, :])
+    gdts[span, :] = grad_dt
+    hsum[0:1] += jnp.sum(dlog * dt, axis=0, keepdims=True) * rate
+    hsum[1:2] += jnp.sum(grad_dt, axis=0, keepdims=True)
     r = dot_nt(gz[now], xb_ref[0])
     turned = jnp.transpose(r[:128] + r[128:])
-    grad_b = part_ref[span, :LANES] + turned[:64] + turned[64:]
-    grad_c = part_ref[span, LANES:]
-    stage[step, :, :lines] = grad_c.reshape(zs, lines, LANES)
-    stage[step, :, lines:] = grad_b.reshape(zs, lines, LANES)
 
     @pl.when(step == 0)
     def _():
-        pl.semaphore_wait(barrier, zs - 1 + flats - 1)
-
-    for d in range(1, zs):
-        scatter(step, d).start()
+        pl.semaphore_wait(barrier, zs - 1 + near - 1 + far - 1)
+
+    total_b.send(step, part_ref[span, :LANES] + turned[:64] + turned[64:])
+
+    @pl.when(step < late)
+    def _():
+        total_c.send(step, part_ref[span, LANES:])
+
+    def reduce(j):
+        total_b.reduce(j)
+
+        @pl.when(j < late)
+        def _():
+            total_c.reduce(j)
+
+    def finish(j):
+        gbc_ref[rows_of(blocks - 1 - j), :LANES] = total_b.result(j)
+
+        @pl.when(j < late)
+        def _():
+            gbc_ref[rows_of(blocks - 1 - j), LANES:] = total_c.result(j)
 
     @pl.when(step >= LAG)
     def _():
-        reduce_pair(step - LAG)
+        reduce(step - LAG)
 
     @pl.when(step >= 2 * LAG)
     def _():
-        finish_pair(step - 2 * LAG)
+        finish(step - 2 * LAG)
 
     @pl.when(step == blocks - 1)
     def _():
-        closing = jnp.concatenate(
-            [jnp.sum(gin_ref[i] * hend_ref[:, c], axis=0, keepdims=True) for i, c in enumerate(chunks)], axis=1)
-        hi, lo = halves(jnp.broadcast_to(closing, (16, width)))
-        totals = dot_nt(hi, sel[...]) + dot_nt(lo, sel[...])
-        after = totals[0:1]
-        gdts = []
-        tri = triangle(True)
-        d_alog = jnp.zeros((1, LANES), F32)
-        d_bias = jnp.zeros((1, LANES), F32)
-        for k in reversed(range(blocks)):
-            span = slice(k * Q, (k + 1) * Q)
-            w = ws[span]
-            dt = dts[span]
-            dlog = dot_nn(tri, vs[span] - w, HIGH) + after
-            after = dlog[0:1]
-            grad_dt = (w / dt + dlog * rate) * jax.nn.sigmoid(shs[span])
-            gdts.append(grad_dt)
-            d_alog = d_alog + jnp.sum(dlog * dt, axis=0, keepdims=True)
-            d_bias = d_bias + jnp.sum(grad_dt, axis=0, keepdims=True)
-        hsum[...] = jnp.concatenate([d_alog * rate, d_bias, dskip_ref[0:1], jnp.zeros((5, LANES), F32)], axis=0)
-
-        @pl.loop(1, flats)
-        def _(d):
-            share(d).start()
-
+        for d in range(1, near):
+            share(d, inner).start()
+        hgot[inner] = hsum[...]
         for j in range(blocks - LAG, blocks):
-            reduce_pair(j)
-        gdt_ref[...] = jnp.transpose(jnp.concatenate(gdts[::-1], axis=0))[:heads]
-        for j in range(blocks - 2 * LAG, blocks - LAG):
-            finish_pair(j)
-        hgot[flat] = hsum[...]
-
-        @pl.loop(1, flats)
-        def _(d):
-            share_in(d).wait_recv()
-
+            total_b.reduce(j)
+        gdt_ref[...] = jnp.transpose(gdts[...])[:heads]
+        for d in range(1, near):
+            share(d, lax.rem(inner + d, near)).wait_recv()
         total = hgot[0]
-        for other in range(1, flats):
+        for other in range(1, near):
             total = total + hgot[other]
+        hmid[...] = total
+        hall[outer] = total
+        for d in range(1, far):
+            spread(d, outer).start()
+        for j in range(blocks - 2 * LAG, blocks):
+            gbc_ref[rows_of(blocks - 1 - j), :LANES] = total_b.result(j)
+        for d in range(1, far):
+            spread(d, lax.rem(outer + d, far)).wait_recv()
+        total = hall[0]
+        for other in range(1, far):
+            total = total + hall[other]
         gheads_ref[...] = total[:3, :heads] * scale
-        for j in range(blocks - LAG, blocks):
-            finish_pair(j)
-
-        @pl.loop(1, flats)
-        def _(d):
-            share(d).wait_send()
-
-        @pl.loop(0, blocks)
-        def _(j):
-            for d in range(1, zs):
-                scatter(j, d).wait_send()
-                gather(j, d).wait_send()
+        for d in range(1, near):
+            share(d, inner).wait_send()
+        for d in range(1, far):
+            spread(d, outer).wait_send()
+        total_b.sent()
+        total_c.sent()
 
 
 def main(heads, y, alog, gin, hend, dskip, part, dts, shs, rows, vs, xs, ls, fs, ab):
@@ -643,7 +687,7 @@
     zs, dps = lax.axis_size("head"), lax.axis_size("dp")
     flats = lax.axis_size("seq") * dps
     scale = 1.0 / math.sqrt(flats * length)
-    lines = Q // zs
+    near = math.gcd(flats, 8)
     dma = pltpu.SemaphoreType.DMA
     whole = pl.BlockSpec(memory_space=pltpu.VMEM)
     back = pl.BlockSpec((Q, width), lambda i: (blocks - 1 - i, 0))
@@ -666,15 +710,13 @@
             pltpu.VMEM((2, 256, width), BF16),
             pltpu.VMEM((128, width), BF16),
             pltpu.VMEM((state, width), F32),
-            pltpu.VMEM((blocks, zs, 2 * lines, state), F32),
-            pltpu.VMEM((blocks, zs, 2 * lines, state), F32),
-            pltpu.VMEM((blocks, zs, 2 * lines, state), F32),
             pltpu.VMEM((8, LANES), F32),
-            pltpu.VMEM((flats, 8, LANES), F32),
-            dma((blocks, zs)), dma((blocks, zs)),
-            dma((blocks, zs)), dma((blocks, zs)),
-            dma((flats,)), dma((flats,)),
-        ],
+            pltpu.VMEM((8, LANES), F32),
+            pltpu.VMEM((near, 8, LANES), F32),
+            pltpu.VMEM((8, LANES), F32),
+            pltpu.VMEM((flats // near, 8, LANES), F32),
+            dma((near,)), dma((near,)), dma((flats // near,)), dma((flats // near,)),
+        ] + head_sum_scratch(blocks, zs) + head_sum_scratch(2 * LAG, zs),
         compiler_params=pltpu.CompilerParams(
             vmem_limit_bytes=VMEM_LIMIT, collective_id=1, has_side_effects=True, dimension_semantics=("arbitrary",)),
         cost_estimate=pl.CostEstimate(flops=60 * length * width * state, bytes_accessed=12 * length * width, transcendentals=0),

time: 120 us -> 122 us (1.017)
  Pallas kernels: 112 us -> 114 us
    pallas_call x1, Pallas kernels: 60.5 us -> 64.5 us  [edges(): pl.pallas_call(functools.partial(edges_kernel, heads), out_shape=(jax.Sha...]
    pallas_call x1, Pallas kernels: 51.6 us -> 50 us  [main(): pl.pallas_call(functools.partial(main_kernel, heads, zs, dps, flats, scal...]
where the time goes in v5:
time: 122 us
  Pallas kernels  114 us (93%)
  local copies, waits for them, and re-layouts  7.1 us (6%)
    pallas_call x1, Pallas kernels, edges(): pl.pallas_call(functools.partial(edges_kernel, heads), out_shape=(jax.Sha...  64.5 us
    pallas_call x1, Pallas kernels, main(): pl.pallas_call(functools.partial(main_kernel, heads, zs, dps, flats, scal...  50 us
    unnamed x10, local copies, waits for them, and re-layouts  7.1 us

profile of v5, /device:TPU:0, one launch (start us, length us, event | category | flops | bytes accessed | tf_op | source)
XLA Modules:
  0.0 122.2 jit_solution(17815691083280447611)
XLA Ops:
  0.6 64.5 %shard_map.102 = (f32[8,128,256]{2,1,0:T(8,128)}, f32[128,2048]{1,0:T(8,128)}, f32[8,128]{1,0:T(8,128)}, f32[1024,256]{1,0:T(8,128)}, f32[1024,128]{1,0:T(8,128)...) custom-call(bf16[1024,2048]{1,0:T(8,128)(2,1)} %bitcast.14, ...), custom_call_target="tpu_custom_call" | custom-call | flops 2147483648 | bytes 8388608 | tf_op jit(solution)/shard_map/pallas_call | solution.py:476
  65.1 50.0 %shard_map.103 = (bf16[1024,2048]{1,0:T(8,128)(2,1)}, f32[1024,256]{1,0:T(8,128)}, f32[32,1024]{1,0:T(8,128)}, f32[3,32]{1,0:T(4,128)}) custom-call(bf16[16,128,2048]{2,1,0:T(8,128)(2,1)} %get-tuple-element.20.xb_ref, bf16[16,128,2048]{2,1,0:T(8,128)(2,1)} %get-tuple-element.21.lb_ref, f32[1024,2048]{1,0:T(8,128)} %get-tuple-element.22.fb_ref, ...), custom_call_target="tpu_custom_call" | custom-call | flops 16106127360 | bytes 25165824 | tf_op jit(solution)/shard_map/pallas_call | solution.py:696
  115.1 0.0 copy-start
  115.1 0.0 copy-start.1
  115.1 0.0 copy-start.2
  115.2 4.9 %copy.15 = bf16[1,1024,2048]{2,1,0:T(8,128)(2,1)} copy(bf16[1,1024,2048]{2,1,0:T(8,128)(2,1)} %bitcast.17) | data formatting | bytes 8388608
  120.0 0.0 copy-done
  120.0 1.0 copy.16
  121.0 0.0 copy-done.1
  121.0 0.7 copy.17
  121.7 0.0 copy-done.2
  121.7 0.6 copy.18
Async XLA Ops:
  115.1 4.9 %copy-start = (f32[1024,256]{1,0:T(8,128)S(1)}, f32[1024,256]{1,0:T(8,128)}, u32[]{:S(2)}) copy-start(f32[1024,256]{1,0:T(8,128)} %get-tuple-element.33) | copy-start | bytes 3145732
  115.1 5.9 %copy-start.1 = (f32[32,1024]{1,0:T(8,128)S(1)}, f32[32,1024]{1,0:T(8,128)}, u32[]{:S(2)}) copy-start(f32[32,1024]{1,0:T(8,128)} %get-tuple-element.34) | copy-start | bytes 393220
  115.1 6.5 %copy-start.2 = (f32[3,32]{1,0:T(4,128)S(1)}, f32[3,32]{1,0:T(4,128)}, u32[]{:S(2)}) copy-start(f32[3,32]{1,0:T(4,128)} %get-tuple-element.43) | copy-start | bytes 1156

commit v6 on v5

--- a/solution.py
+++ b/solution.py
@@ -9,7 +9,7 @@
 from jax.sharding import PartitionSpec as P
 
 Q = 64
-LAG = 3
+LAG = 4
 CHUNK = 256
 HEADDIM = 64
 LANES = 128
@@ -114,7 +114,7 @@
         for d in range(1, self.zs):
             q = self.peer(d)
             self.copy(self.done.at[j, q], self.done.at[j, q], self.s2.at[j, q], self.r2.at[j, q], q).wait_recv()
-        return self.done[j].reshape(Q, LANES)
+        return self.done[j].reshape(-1, LANES)
 
     def sent(self):
         @pl.loop(0, self.stage.shape[0])
@@ -124,8 +124,8 @@
                 self.gather(j, d).wait_send()
 
 
-def head_sum_scratch(count, zs):
-    buffer = pltpu.VMEM((count, zs, Q // zs, LANES), F32)
+def head_sum_scratch(count, zs, lines):
+    buffer = pltpu.VMEM((count, zs, lines, LANES), F32)
     return [buffer] * 3 + [pltpu.SemaphoreType.DMA((count, zs))] * 4
 
 
@@ -139,8 +139,7 @@
                  gin_ref, hst, skip_ref, part, dts, shs, rows, vs, xo_ref, lo_ref, fo_ref, ab_ref,
                  pe, pf, le, lf, bt, ct, sel, xb, yb, xs, dec, out0, got0, chip, gath, pre, inc, fin,
                  xbuf, lbuf, fbuf, abuf, bbuf, yx, hz,
-                 load_sem, s0, r0, s1, r1, s2, r2, s3, r3, put_sem, put_one,
-                 stage, landed, done, z1, z2, z3, z4):
+                 load_sem, s0, r0, s1, r1, s2, r2, s3, r3, put_sem, put_one):
     length = bc_ref.shape[0]
     blocks = length // Q
     groups = gin_ref.shape[0]
@@ -194,10 +193,7 @@
     for i in range(groups):
         for copy in loads(i):
             copy.start()
-    total_c = HeadSum(stage, landed, done, (z1, z2, z3, z4))
-    early = stage.shape[0]
     barrier = pltpu.get_barrier_semaphore()
-    greet_heads(barrier, total_c.zs)
     pl.semaphore_signal(barrier, inc=1, device_id={"seq": partner}, device_id_type=pl.DeviceIdType.MESH)
     for d in range(1, groups):
         pl.semaphore_signal(barrier, inc=1, device_id={"seq": peer(d) * 2 + core}, device_id_type=pl.DeviceIdType.MESH)
@@ -229,7 +225,7 @@
     bt[:, length:] = b_t
     ct[:, :length] = c_t
     ct[:, length:] = c_t
-    pl.semaphore_wait(barrier, groups + total_c.zs - 1)
+    pl.semaphore_wait(barrier, groups)
 
     def combine(i):
         swap(i).wait_recv()
@@ -416,21 +412,7 @@
         vs[span, :] = sums[0:64] + sums[64:128]
         r = dot_nt(hz[now], lbuf[k])
         turned = jnp.transpose(r[:128] + r[128:])
-        grad_c = part[span, LANES:] + turned[:64] + turned[64:]
-        part[span, LANES:] = grad_c
-
-        @pl.when(k < early)
-        def _():
-            total_c.send(k, grad_c)
-
-        @pl.when((k >= LAG) & (k < early + LAG))
-        def _():
-            total_c.reduce(k - LAG)
-
-        @pl.when(k >= 2 * LAG)
-        def _():
-            j = k - 2 * LAG
-            part[pl.ds(pl.multiple_of(j * Q, Q), Q), LANES:] = total_c.result(j)
+        part[span, LANES:] += turned[:64] + turned[64:]
 
         @pl.when((k == blocks // 4) & behind)
         def _():
@@ -461,7 +443,6 @@
         for copy in puts(i):
             copy.wait()
     put_ab.wait()
-    total_c.sent()
 
 
 def edges(x, y, bc, dt, bias, alog, skip):
@@ -523,7 +504,7 @@
             dma((groups,)), dma((groups,)),
             dma((groups,)), dma((groups,)),
             dma((3, groups)), dma,
-        ] + head_sum_scratch(blocks - 2 * LAG, lax.axis_size("head")),
+        ],
         compiler_params=pltpu.CompilerParams(vmem_limit_bytes=VMEM_LIMIT, collective_id=0, has_side_effects=True),
         cost_estimate=pl.CostEstimate(flops=8 * length * width * state, bytes_accessed=4 * length * width, transcendentals=0),
     )(x, y, bc, dt, bias, alog, skip)
@@ -541,9 +522,8 @@
     kb = blocks - 1 - step
     chunks = [slice(c * CHUNK, (c + 1) * CHUNK) for c in range(width // CHUNK)]
     rate = rates_of(alog_ref, heads)
-    total_b = HeadSum(b_stage, b_landed, b_done, (b1, b2, b3, b4))
     total_c = HeadSum(c_stage, c_landed, c_done, (c1, c2, c3, c4))
-    late = c_stage.shape[0]
+    z = lax.axis_index("head")
     flat = lax.axis_index("seq") * dps + lax.axis_index("dp")
     near = hgot.shape[0]
     far = hall.shape[0]
@@ -585,7 +565,6 @@
         hi, lo = halves(jnp.broadcast_to(closing, (16, width)))
         carry[...] = (dot_nt(hi, sel[...]) + dot_nt(lo, sel[...]))[:8]
         hsum[...] = jnp.where(iota(hsum.shape, 0) == 2, dskip_ref[...], 0.0)
-        gbc_ref[:(blocks - late) * Q, LANES:] = part_ref[:(blocks - late) * Q, LANES:]
 
     span = pl.ds(pl.multiple_of(kb * Q, Q), Q)
     now = lax.rem(step, 2)
@@ -619,25 +598,56 @@
     def _():
         pl.semaphore_wait(barrier, zs - 1 + near - 1 + far - 1)
 
-    total_b.send(step, part_ref[span, :LANES] + turned[:64] + turned[64:])
-
-    @pl.when(step < late)
-    def _():
-        total_c.send(step, part_ref[span, LANES:])
-
-    def reduce(j):
-        total_b.reduce(j)
-
-        @pl.when(j < late)
+        total_c.send(0, part_ref[:, LANES:])
+
+    def owner(t):
+        return lax.rem(blocks - 1 - t, zs)
+
+    def to_owner(t, source):
+        j = t // zs
+        return pltpu.make_async_remote_copy(
+            src_ref=b_stage.at[t], dst_ref=b_landed.at[j, source], send_sem=b1.at[t], recv_sem=b2.at[j, source],
+            device_id={"head": owner(t)}, device_id_type=pl.DeviceIdType.MESH)
+
+    def from_owner(t, dest):
+        return pltpu.make_async_remote_copy(
+            src_ref=b_done.at[t], dst_ref=b_done.at[t], send_sem=b3.at[t, dest], recv_sem=b4.at[t],
+            device_id={"head": dest}, device_id_type=pl.DeviceIdType.MESH)
+
+    def reduce(t):
+        @pl.when(owner(t) == z)
         def _():
-            total_c.reduce(j)
-
-    def finish(j):
-        gbc_ref[rows_of(blocks - 1 - j), :LANES] = total_b.result(j)
-
-        @pl.when(j < late)
+            j = t // zs
+            for d in range(1, zs):
+                source = lax.rem(z + d, zs)
+                pltpu.make_async_remote_copy(
+                    src_ref=b_stage.at[t], dst_ref=b_landed.at[j, source], send_sem=b1.at[t],
+                    recv_sem=b2.at[j, source], device_id={"head": source},
+                    device_id_type=pl.DeviceIdType.MESH).wait_recv()
+            b_landed[j, z] = b_stage[t]
+            total = b_landed[j, 0]
+            for other in range(1, zs):
+                total = total + b_landed[j, other]
+            b_done[t] = total
+            for d in range(1, zs):
+                from_owner(t, lax.rem(z + d, zs)).start()
+
+    def finish(t):
+        @pl.when(owner(t) != z)
         def _():
-            gbc_ref[rows_of(blocks - 1 - j), LANES:] = total_c.result(j)
+            from_owner(t, owner(t)).wait_recv()
+
+        gbc_ref[rows_of(blocks - 1 - t), :LANES] = b_done[t]
+
+    b_stage[step] = part_ref[span, :LANES] + turned[:64] + turned[64:]
+
+    @pl.when(owner(step) != z)
+    def _():
+        to_owner(step, z).start()
+
+    @pl.when(step == blocks // 2)
+    def _():
+        total_c.reduce(0)
 
     @pl.when(step >= LAG)
     def _():
@@ -652,8 +662,8 @@
         for d in range(1, near):
             share(d, inner).start()
         hgot[inner] = hsum[...]
-        for j in range(blocks - LAG, blocks):
-            total_b.reduce(j)
+        for t in range(blocks - LAG, blocks):
+            reduce(t)
         gdt_ref[...] = jnp.transpose(gdts[...])[:heads]
         for d in range(1, near):
             share(d, lax.rem(inner + d, near)).wait_recv()
@@ -664,8 +674,9 @@
         hall[outer] = total
         for d in range(1, far):
             spread(d, outer).start()
-        for j in range(blocks - 2 * LAG, blocks):
-            gbc_ref[rows_of(blocks - 1 - j), :LANES] = total_b.result(j)
+        gbc_ref[:, LANES:] = total_c.result(0)
+        for t in range(blocks - 2 * LAG, blocks):
+            finish(t)
         for d in range(1, far):
             spread(d, lax.rem(outer + d, far)).wait_recv()
         total = hall[0]
@@ -676,8 +687,18 @@
             share(d, inner).wait_send()
         for d in range(1, far):
             spread(d, outer).wait_send()
-        total_b.sent()
         total_c.sent()
+
+        @pl.loop(0, blocks)
+        def _(t):
+            @pl.when(owner(t) != z)
+            def _():
+                to_owner(t, z).wait_send()
+
+            @pl.when(owner(t) == z)
+            def _():
+                for d in range(1, zs):
+                    from_owner(t, lax.rem(z + d, zs)).wait_send()
 
 
 def main(heads, y, alog, gin, hend, dskip, part, dts, shs, rows, vs, xs, ls, fs, ab):
@@ -716,7 +737,11 @@
             pltpu.VMEM((8, LANES), F32),
             pltpu.VMEM((flats // near, 8, LANES), F32),
             dma((near,)), dma((near,)), dma((flats // near,)), dma((flats // near,)),
-        ] + head_sum_scratch(blocks, zs) + head_sum_scratch(2 * LAG, zs),
+            pltpu.VMEM((blocks, Q, LANES), F32),
+            pltpu.VMEM((blocks // zs, zs, Q, LANES), F32),
+            pltpu.VMEM((blocks, Q, LANES), F32),
+            dma((blocks,)), dma((blocks // zs, zs)), dma((blocks, zs)), dma((blocks,)),
+        ] + head_sum_scratch(1, zs, length // zs),
         compiler_params=pltpu.CompilerParams(
             vmem_limit_bytes=VMEM_LIMIT, collective_id=1, has_side_effects=True, dimension_semantics=("arbitrary",)),
         cost_estimate=pl.CostEstimate(flops=60 * length * width * state, bytes_accessed=12 * length * width, transcendentals=0),

time: 122 us -> 120 us (0.984)
  Pallas kernels: 114 us -> 112 us
    pallas_call x1, Pallas kernels: 64.5 us -> 60.7 us  [edges(): pl.pallas_call(functools.partial(edges_kernel, heads), out_shape=(jax.Sha...]
where the time goes in v6:
time: 120 us
  Pallas kernels  112 us (93%)
  local copies, waits for them, and re-layouts  7.1 us (6%)
    pallas_call x1, Pallas kernels, edges(): pl.pallas_call(functools.partial(edges_kernel, heads), out_shape=(jax.Sha...  60.7 us
    pallas_call x1, Pallas kernels, main(): pl.pallas_call(functools.partial(main_kernel, heads, zs, dps, flats, scal...  51.2 us
    unnamed x10, local copies, waits for them, and re-layouts  7.1 us

profile of v6, /device:TPU:0, one launch (start us, length us, event | category | flops | bytes accessed | tf_op | source)
XLA Modules:
  0.0 119.6 jit_solution(1507933870671620917)
XLA Ops:
  0.6 60.7 %shard_map.102 = (f32[8,128,256]{2,1,0:T(8,128)}, f32[128,2048]{1,0:T(8,128)}, f32[8,128]{1,0:T(8,128)}, f32[1024,256]{1,0:T(8,128)}, f32[1024,128]{1,0:T(8,128)...) custom-call(bf16[1024,2048]{1,0:T(8,128)(2,1)} %bitcast.14, ...), custom_call_target="tpu_custom_call" | custom-call | flops 2147483648 | bytes 8388608 | tf_op jit(solution)/shard_map/pallas_call | solution.py:457
  61.3 51.2 %shard_map.103 = (bf16[1024,2048]{1,0:T(8,128)(2,1)}, f32[1024,256]{1,0:T(8,128)}, f32[32,1024]{1,0:T(8,128)}, f32[3,32]{1,0:T(4,128)}) custom-call(bf16[16,128,2048]{2,1,0:T(8,128)(2,1)} %get-tuple-element.20.xb_ref, bf16[16,128,2048]{2,1,0:T(8,128)(2,1)} %get-tuple-element.21.lb_ref, f32[1024,2048]{1,0:T(8,128)} %get-tuple-element.22.fb_ref, ...), custom_call_target="tpu_custom_call" | custom-call | flops 16106127360 | bytes 25165824 | tf_op jit(solution)/shard_map/pallas_call | solution.py:717
  112.5 0.0 copy-start
  112.5 0.0 copy-start.1
  112.5 0.0 copy-start.2
  112.5 4.9 %copy.15 = bf16[1,1024,2048]{2,1,0:T(8,128)(2,1)} copy(bf16[1,1024,2048]{2,1,0:T(8,128)(2,1)} %bitcast.17) | data formatting | bytes 8388608
  117.4 0.0 copy-done
  117.4 1.0 copy.16
  118.4 0.0 copy-done.1
  118.4 0.7 copy.17
  119.0 0.0 copy-done.2
  119.0 0.6 copy.18
Async XLA Ops:
  112.5 4.9 %copy-start = (f32[1024,256]{1,0:T(8,128)S(1)}, f32[1024,256]{1,0:T(8,128)}, u32[]{:S(2)}) copy-start(f32[1024,256]{1,0:T(8,128)} %get-tuple-element.33) | copy-start | bytes 3145732
  112.5 5.9 %copy-start.1 = (f32[32,1024]{1,0:T(8,128)S(1)}, f32[32,1024]{1,0:T(8,128)}, u32[]{:S(2)}) copy-start(f32[32,1024]{1,0:T(8,128)} %get-tuple-element.34) | copy-start | bytes 393220
  112.5 6.5 %copy-start.2 = (f32[3,32]{1,0:T(4,128)S(1)}, f32[3,32]{1,0:T(4,128)}, u32[]{:S(2)}) copy-start(f32[3,32]{1,0:T(4,128)} %get-tuple-element.43) | copy-start | bytes 1156
